TPU v7x, 32 devices: a whole 2x2x4 slice. The times are simulated.
32 devices in a mesh: section: 2 (over y), len: 4 (over z), ht: 2 (over x), wd: 2 (over core).
Axes of the slice: x: 2, y: 2, z: 4, core: 2. Of those that a mesh axis runs over, the one named last changes fastest.
Arguments:
- positions: float32 [3, 64, 4, 4, 128], P(None, ('section', 'len'), 'ht', 'wd'), parts along dimension 1, may hold values from 0 to 1
- velocities: float32 [3, 64, 4, 4, 128], P(None, ('section', 'len'), 'ht', 'wd'), parts along dimension 1, may hold values from -3 to 3
- radius: float32 [64, 4, 4, 128], P(('section', 'len'), 'ht', 'wd'), parts along dimension 0, may hold values from 0.3 to 0.6
- counts: int32 [64, 4, 4], P(('section', 'len'), 'ht', 'wd'), parts along dimension 0, may hold values from 0 to 128, as said below
- cell_index: int32 [64, 4, 4, 128], P(('section', 'len'), 'ht', 'wd'), parts along dimension 0, may hold values from 0 to 1023
- fluid_velocity: float32 [3, 8192], P(None, ('section', 'len', 'ht', 'wd')), parts along dimension 1, may hold values from -6 to 6
- plan: int32 [8, 2, 2, 32, 1], P(('section', 'len'), 'ht', 'wd'), parts along dimension 0, may hold values from 0 to 3; in each aligned block of 32 rows (0 to 31, 32 to 63, ..., all dimensions but the last counted through in order) at most 16 rows name the same one
Outputs:
- moved: float32 [8, 2, 2, 512, 128], P(None, 'ht', 'wd', ('section', 'len')), parts along dimension 3
- fluid_next: float32 [3, 8192], P(None, ('section', 'len', 'ht', 'wd')), parts along dimension 1
There are 2 independent parts, one for each index of `section`. A program takes and returns all parts, laid end to end along the dimension named above; each array names one. Nothing has to cross between parts.
Inputs may be any that keep to these rules, and one draw needn't show every extreme that they name: `plan`: within the bins of one device no destination is named by more than 16 bins, and on some devices one is named by exactly 16. `counts`: about a third of the bins are full.
All inputs are finite; a program needn't handle non-finite values.
Results may differ from a plain program's by a relative error of at most 0.0003.
Values sent between devices are 32-bit elements; how exact they have to be, the bound alone decides.
A program may use at most 64 MiB of HBM per device.

v0:
```python
import jax
import jax.numpy as jnp
from jax import lax
from jax.sharding import PartitionSpec as P

SUBSTEPS = 2


STEP = 0.1
STIFF = 1.0
COUPLE = 0.5
RADIUS_REF = 0.45
OFFSETS = ((0, 0, 0), (1, 0, 0), (-1, 0, 0), (0, 1, 0), (0, -1, 0), (0, 0, 1), (0, 0, -1))
HIGHEST = lax.Precision.HIGHEST


def padded_2(block, sides, width):
    for axis, dim in sides:
        count = lax.axis_size(axis)
        forward = [(i, i + 1) for i in range(count - 1)]
        backward = [(target, source) for source, target in forward]
        low = lax.ppermute(
            lax.slice_in_dim(block, block.shape[dim] - width, None, axis=dim), axis, forward
        )
        high = lax.ppermute(lax.slice_in_dim(block, 0, width, axis=dim), axis, backward)
        block = jnp.concatenate([low, block, high], axis=dim)
    return block


def contact_forces(padded):
    rows = padded.shape[1] - 2
    heights = padded.shape[2] - 2
    widths = padded.shape[3] - 2
    shifts = jnp.array(OFFSETS, dtype=jnp.float32).T.reshape(3, 7, 1, 1, 1)

    def one_row(index):
        slab = lax.dynamic_slice_in_dim(padded, index, 3, 1)
        centre = slab[:, 1, 1 : heights + 1, 1 : widths + 1, :]
        pieces = []
        for da, db, dc in OFFSETS:
            pieces.append(slab[:, 1 + da, 1 + db : 1 + db + heights, 1 + dc : 1 + dc + widths, :])
        sources = jnp.stack(pieces, axis=1)
        source_pos = sources[:3] + shifts
        diff = source_pos[:, :, :, :, None, :] - centre[:3][:, None, :, :, :, None]
        dist = jnp.sum(diff * diff, axis=0)
        reach = sources[3][:, :, :, None, :] + centre[3][None, :, :, :, None]
        weight = sources[4][:, :, :, None, :] * jnp.exp(-dist / (reach * reach))
        return -STIFF * jnp.sum(weight[None] * diff, axis=(1, 5))

    forces = lax.map(one_row, jnp.arange(rows, dtype=jnp.int32))
    return jnp.moveaxis(forces, 0, 1)


def position_rim(place):
    return padded_2(place, (("len", 1), ("ht", 2), ("wd", 3)), 1)


def per_device(positions, velocities, radius, counts, cell_index, fluid_velocity, plan):
    slots = radius.shape[-1]
    live = (jnp.arange(slots, dtype=jnp.int32)[None, None, None, :] < counts[..., None]).astype(
        jnp.float32
    )
    mass = (radius / RADIUS_REF) ** 3
    cells = cell_index.reshape(-1)
    total = cells.shape[0]
    width = fluid_velocity.shape[1]
    groups = lax.axis_size(("ht", "wd"))
    piece = lax.all_gather(fluid_velocity, ("ht", "wd"), axis=1, tiled=True)
    count = piece.shape[1]
    onehot = (cells[:, None] == jnp.arange(count, dtype=jnp.int32)[None, :]).astype(jnp.float32)
    fluid_here = jnp.einsum("cf,pf->cp", piece, onehot, precision=HIGHEST)
    fluid_here = fluid_here.reshape(velocities.shape)
    props = padded_2(jnp.stack([radius, live]), (("len", 1), ("ht", 2), ("wd", 3)), 1)
    place = positions
    speed = velocities
    acc = jnp.zeros_like(velocities)
    for step in range(SUBSTEPS):
        padded = jnp.concatenate([position_rim(place), props], axis=0)
        force = contact_forces(padded)
        drag = radius * (fluid_here - speed)
        acc = acc + drag
        speed = speed + STEP * (force + drag) / mass
        place = place + STEP * speed
    term = jnp.concatenate([acc * live, (mass * live)[None]], axis=0).reshape(4, total)

    def cell_block(start):
        onehot = (cells[:, None] == (start + jnp.arange(width, dtype=jnp.int32))[None, :]).astype(
            jnp.float32
        )
        return jnp.einsum("cp,pf->cf", term, onehot, precision=HIGHEST)

    blocks = lax.map(cell_block, jnp.arange(groups, dtype=jnp.int32) * width)
    partial_sums = blocks.transpose(1, 0, 2).reshape(4, groups * width)
    sums = lax.psum_scatter(partial_sums, ("ht", "wd"), scatter_dimension=1, tiled=True)
    fluid_next = fluid_velocity - COUPLE * sums[:3] / (1.0 + sums[3:4])
    bins = counts.size
    length_peers = lax.axis_size("len")
    cap = max(2, 2 * bins // length_peers)
    state = jnp.concatenate([place * live, speed * live, (radius * live)[None], live[None]], axis=0)
    flat = state.reshape(8, bins, slots)
    dest = plan.reshape(bins)
    order = jnp.arange(bins, dtype=jnp.int32)
    same = dest[:, None] == dest[None, :]
    earlier = order[None, :] < order[:, None]
    rank = jnp.sum((same & earlier).astype(jnp.int32), axis=1)
    slot = dest * cap + rank
    select = slot[None, :] == jnp.arange(length_peers * cap, dtype=jnp.int32)[:, None]
    outgoing = jnp.einsum("cbp,sb->csp", flat, select.astype(jnp.float32), precision=HIGHEST)
    arrived = lax.all_to_all(outgoing, "len", split_axis=1, concat_axis=1, tiled=True)
    moved = arrived.reshape(8, 1, 1, length_peers * cap, slots)
    return (moved, fluid_next)


def solution(mesh):
    in_specs = (
        P(None, ("section", "len"), "ht", "wd", None),
        P(None, ("section", "len"), "ht", "wd", None),
        P(("section", "len"), "ht", "wd", None),
        P(("section", "len"), "ht", "wd"),
        P(("section", "len"), "ht", "wd", None),
        P(None, ("section", "len", "ht", "wd")),
        P(("section", "len"), "ht", "wd", None, None),
    )
    out_specs = (
        P(None, "ht", "wd", ("section", "len"), None),
        P(None, ("section", "len", "ht", "wd")),
    )
    return jax.shard_map(
        per_device, mesh=mesh, in_specs=in_specs, out_specs=out_specs, check_vma=False
    )
```

profile of v0, /device:TPU:0, one launch (start us, length us, event | category | flops | bytes accessed | tf_op | source)
XLA Modules:
  0.0 208.5 jit_solution(15648498818927893236)
XLA Ops:
  8.7 4.9 %collective-permute-start.6 = (f32[2,1,2,2,128]{4,1,3,2,0:T(1,128)S(1)}, f32[2,1,2,2,128]{4,1,3,2,0:T(1,128)S(1)}, u32[]{:S(2)}, u32[]{:S(2)}) collective-permute-start(f32[2,1,2,2,128]{4,1,3,2,0:T(1,128)S(1)} %get-tuple-element.191), channel_id=1, source_target_pairs={{0,4},{4,8},{8,12},{1,5},{5,9},{9,13},{2,6},{6,10},{10,14},{3,7},{... | collective-permute-start | bytes 12296 | tf_op jit(solution)/shard_map/ppermute | solution.py:22
  13.6 1.3 collective-permute-start.7
  15.6 4.5 %collective-permute-start = (f32[3,1,2,2,128]{4,3,2,1,0:T(2,128)S(1)}, f32[3,1,2,2,128]{4,3,2,1,0:T(2,128)S(1)}, u32[]{:S(2)}, u32[]{:S(2)}) collective-permute-start(f32[3,1,2,2,128]{4,3,2,1,0:T(2,128)S(1)} %get-tuple-element.190), channel_id=1, source_target_pairs={{0,4},{4,8},{8,12},{1,5},{5,9},{9,13},{2,6},{6,10},{10,14},{3,7},{... | collective-permute-start | bytes 18440 | tf_op jit(solution)/shard_map/ppermute | solution.py:22
  20.2 1.3 collective-permute-start.1
  23.2 5.3 %all_gather.3 = f32[3,1024]{1,0:T(4,128)S(1)} all-gather(f32[3,256]{1,0:T(4,128)} %param.20), channel_id=1, replica_groups=mesh['section'=2,'len'=4,'ht'=2,'wd'=2] {'ht','wd'}, dimensions={1}, use_global_device_ids=true | all-gather | bytes 15360 | tf_op jit(solution)/shard_map/all_gather | solution.py:68
  28.6 8.7 %fusion.20 = f32[3,4096]{1,0:T(4,128)S(1)} fusion(f32[3,1024]{1,0:T(4,128)S(1)} %all_gather.3, s32[4096]{0:T(1024)} %bitcast.130), kind=kOutput, calls=%fused_computation.46 | convolution fusion | flops 155189248 | bytes 77824 | tf_op jit(solution)/shard_map/cf,pf->cp/dot_general | solution.py:71
  37.5 3.4 %collective-permute-start.8 = (f32[2,10,1,2,128]{4,1,3,2,0:T(8,128)S(1)}, f32[2,10,1,2,128]{4,1,3,2,0:T(8,128)S(1)}, u32[]{:S(2)}, u32[]{:S(2)}) collective-permute-start(f32[2,10,1,2,128]{4,1,3,2,0:T(8,128)S(1)} %get-tuple-element.183), channel_id=1, source_target_pairs={{0,2},{1,3},{4,6},{5,7},{8,10},{9,11},{12,14},{13,15},{16,18},{17,... | collective-permute-start | bytes 61448 | tf_op jit(solution)/shard_map/ppermute | solution.py:22
  40.9 1.3 collective-permute-start.9
  42.3 4.5 %collective-permute-start.2 = (f32[3,10,1,2,128]{4,3,2,1,0:T(2,128)S(1)}, f32[3,10,1,2,128]{4,3,2,1,0:T(2,128)S(1)}, u32[]{:S(2)}, u32[]{:S(2)}) collective-permute-start(f32[3,10,1,2,128]{4,3,2,1,0:T(2,128)S(1)} %get-tuple-element.185), channel_id=1, source_target_pairs={{0,2},{1,3},{4,6},{5,7},{8,10},{9,11},{12,14},{13,15},{16,18},{17,... | collective-permute-start | bytes 92168 | tf_op jit(solution)/shard_map/ppermute | solution.py:22
  46.9 1.3 collective-permute-start.3
  48.2 1.4 collective-permute-start.10
  49.6 1.3 collective-permute-start.11
  50.9 1.7 collective-permute-done.3
  52.8 1.3 collective-permute-start.4
  54.1 1.3 collective-permute-start.5
  55.6 1.7 collective-permute-done.5
  57.6 41.2 %while.33 = (s32[]{:T(128)}, f32[8,3,2,2,128]{4,0,3,2,1:T(8,128)S(1)}, s32[8]{0:T(128)S(1)}, f32[5,10,4,4,128]{4,3,2,1,0:T(4,128)S(1)}, s32[]{:T(128)}, /*index=...) while((s32[]{:T(128)}, f32[8,3,2,2,128]{4,0,3,2,1:T(8,128)S(1)}, ...), condition=%wide.region_4.5_spmd.clone, body=%wide.region_1.4_spmd.clone.sunk | while | flops 10103305 | bytes 7803247 | solution.py:50
  61.8 0.8 fusion.66
  66.9 0.8 fusion.66
  72.1 0.8 fusion.66
  77.2 0.8 fusion.66
  82.4 0.8 fusion.66
  87.5 0.8 fusion.66
  92.7 0.8 fusion.66
  97.8 0.8 fusion.66
  98.8 4.5 %collective-permute-start.12 = (f32[3,1,2,2,128]{4,1,3,2,0:T(1,128)S(1)}, f32[3,1,2,2,128]{4,1,3,2,0:T(1,128)S(1)}, u32[]{:S(2)}, u32[]{:S(2)}) collective-permute-start(f32[3,1,2,2,128]{4,1,3,2,0:T(1,128)S(1)} %get-tuple-element.187), channel_id=1, source_target_pairs={{0,4},{4,8},{8,12},{1,5},{5,9},{9,13},{2,6},{6,10},{10,14},{3,7},{... | collective-permute-start | bytes 18440 | tf_op jit(solution)/shard_map/ppermute | solution.py:22
  103.3 1.3 collective-permute-start.13
  104.8 4.0 %collective-permute-done.13 = f32[3,1,2,2,128]{4,1,3,2,0:T(1,128)S(1)} collective-permute-done((f32[3,1,2,2,128]{4,1,3,2,0:T(1,128)S(1)}, f32[3,1,2,2,128]{4,1,3,2,0:T(1,128)S(1)}, u32[]{:S(2)}, u32[]{:S(2)}) %collective-permute-start.13) | collective-permute-done | bytes 6176 | tf_op jit(solution)/shard_map/ppermute | solution.py:25
  108.9 4.5 %collective-permute-start.14 = (f32[3,10,1,2,128]{4,1,3,2,0:T(8,128)S(1)}, f32[3,10,1,2,128]{4,1,3,2,0:T(8,128)S(1)}, u32[]{:S(2)}, u32[]{:S(2)}) collective-permute-start(f32[3,10,1,2,128]{4,1,3,2,0:T(8,128)S(1)} %get-tuple-element.181), channel_id=1, source_target_pairs={{0,2},{1,3},{4,6},{5,7},{8,10},{9,11},{12,14},{13,15},{16,18},{17,... | collective-permute-start | bytes 92168 | tf_op jit(solution)/shard_map/ppermute | solution.py:22
  113.4 1.3 collective-permute-start.15
  115.1 4.3 %collective-permute-done.15 = f32[3,10,1,2,128]{4,1,3,2,0:T(8,128)S(1)} collective-permute-done((f32[3,10,1,2,128]{4,1,3,2,0:T(8,128)S(1)}, f32[3,10,1,2,128]{4,1,3,2,0:T(8,128)S(1)}, u32[]{:S(2)}, u32[]{:S(2)}) %collective-permute-start.15) | collective-permute-done | bytes 30752 | tf_op jit(solution)/shard_map/ppermute | solution.py:25
  119.4 1.3 collective-permute-start.16
  120.7 1.3 collective-permute-start.17
  122.1 1.9 collective-permute-done.17
  124.2 41.2 %while.34 = (s32[]{:T(128)}, f32[8,3,2,2,128]{4,0,3,2,1:T(8,128)S(1)}, s32[8]{0:T(128)S(1)}, f32[5,10,4,4,128]{4,3,2,1,0:T(4,128)S(1)}, s32[]{:T(128)}, /*index=...) while((s32[]{:T(128)}, f32[8,3,2,2,128]{4,0,3,2,1:T(8,128)S(1)}, ...), condition=%wide.region_8.9_spmd.clone, body=%wide.region_5.8_spmd.clone.sunk | while | flops 10103305 | bytes 7803247 | solution.py:50
  128.4 0.8 fusion.68
  133.6 0.8 fusion.68
  165.6 10.4 %while.32 = (s32[]{:T(128)}, f32[4,4,256]{2,1,0:T(4,128)S(1)}, s32[8,2,2,128]{3,2,1,0:T(2,128)S(1)}, s32[4]{0:T(128)S(1)}, f32[4,4096]{1,0:T(4,128)S(1)}, /*index=5*/s32[]{:T(128)}) while((s32[]{:T(128)}, f32[4,4,256]{2,1,0:T(4,128)S(1)}, s32[8,2,2,128]{3,2,1,0:T(2,128)S(1)}, s32[4]{0:T(128)S(1)}, f32[4,4096]{1,0:T(4,128)S(1)}, ...), condition=%wide.region_10.11_spmd, body=%wide.region_9.10_spmd.sunk | while | flops 51380480 | bytes 88153 | solution.py:92
  166.8 1.4 fusion.64
  169.4 1.4 fusion.64
  172.0 1.4 fusion.64
  174.7 1.4 fusion.64
  176.0 1.1 copy.110
  177.6 0.9 copy.106
  178.4 3.9 %all-to-all-start = ((f32[8,64,128]{2,0,1:T(8,128)}), f32[8,64,128]{2,0,1:T(8,128)S(1)}, u32[]{:S(2)}, u32[]{:S(2)}) async-start(f32[8,64,128]{2,0,1:T(8,128)} %copy.106), calls=%async_computation | async-start | bytes 524288 | tf_op jit(solution)/shard_map/all_to_all | solution.py:109
  182.3 15.9 %reduce-scatter.4.cloned.1.call-done = f32[256,4]{1,0:T(8,128)} async-done(((f32[1024,4]{1,0:T(8,128)}), f32[256,4]{1,0:T(8,128)}) %reduce-scatter.4.cloned.1.call-update) | async-done | bytes 4112
  198.2 1.0 slice_add_fusion.2
  199.3 1.0 copy.116
  (334 shorter events, 52.4 us)
Async XLA Ops:
  7.2 191.1 %reduce-scatter.4.cloned.1.call-start = ((), (), s32[]{:S(2)}) async-start(), calls=%async_computation.2 | async-start | bytes 655360
  8.7 28.8 %collective-permute-start.6 = (f32[2,1,2,2,128]{4,1,3,2,0:T(1,128)S(1)}, f32[2,1,2,2,128]{4,1,3,2,0:T(1,128)S(1)}, u32[]{:S(2)}, u32[]{:S(2)}) collective-permute-start(f32[2,1,2,2,128]{4,1,3,2,0:T(1,128)S(1)} %get-tuple-element.191), channel_id=1, source_target_pairs={{0,4},{4,8},{8,12},{1,5},{5,9},{9,13},{2,6},{6,10},{10,14},{3,7},{... | collective-permute-start | bytes 12296 | tf_op jit(solution)/shard_map/ppermute | solution.py:22
  13.6 23.8 %collective-permute-start.7 = (f32[2,1,2,2,128]{4,1,3,2,0:T(1,128)S(1)}, f32[2,1,2,2,128]{4,1,3,2,0:T(1,128)S(1)}, u32[]{:S(2)}, u32[]{:S(2)}) collective-permute-start(f32[2,1,2,2,128]{4,1,3,2,0:T(1,128)S(1)} %get-tuple-element.192), channel_id=1, source_target_pairs={{4,0},{8,4},{12,8},{5,1},{9,5},{13,9},{6,2},{10,6},{14,10},{7,3},{... | collective-permute-start | bytes 12296 | tf_op jit(solution)/shard_map/ppermute | solution.py:25
  15.6 26.6 %collective-permute-start = (f32[3,1,2,2,128]{4,3,2,1,0:T(2,128)S(1)}, f32[3,1,2,2,128]{4,3,2,1,0:T(2,128)S(1)}, u32[]{:S(2)}, u32[]{:S(2)}) collective-permute-start(f32[3,1,2,2,128]{4,3,2,1,0:T(2,128)S(1)} %get-tuple-element.190), channel_id=1, source_target_pairs={{0,4},{4,8},{8,12},{1,5},{5,9},{9,13},{2,6},{6,10},{10,14},{3,7},{... | collective-permute-start | bytes 18440 | tf_op jit(solution)/shard_map/ppermute | solution.py:22
  20.2 22.1 %collective-permute-start.1 = (f32[3,1,2,2,128]{4,3,2,1,0:T(2,128)S(1)}, f32[3,1,2,2,128]{4,3,2,1,0:T(2,128)S(1)}, u32[]{:S(2)}, u32[]{:S(2)}) collective-permute-start(f32[3,1,2,2,128]{4,3,2,1,0:T(2,128)S(1)} %get-tuple-element.189), channel_id=1, source_target_pairs={{4,0},{8,4},{12,8},{5,1},{9,5},{13,9},{6,2},{10,6},{14,10},{7,3},{... | collective-permute-start | bytes 18440 | tf_op jit(solution)/shard_map/ppermute | solution.py:25
  28.6 13.7 %copy-start = (f32[3,8,2,2,128]{4,3,2,1,0:T(2,128)S(1)}, f32[3,8,2,2,128]{4,3,2,1,0:T(2,128)}, u32[]{:S(2)}) copy-start(f32[3,8,2,2,128]{4,3,2,1,0:T(2,128)} %param.15) | copy-start | bytes 147460
  37.3 20.2 %copy-start.1 = (f32[3,7]{1,0:T(4,128)S(1)}, f32[3,7]{1,0:T(4,128)}, u32[]{:S(2)}) copy-start(f32[3,7]{1,0:T(4,128)} %constant.225) | copy-start | bytes 256
  37.5 10.7 %collective-permute-start.8 = (f32[2,10,1,2,128]{4,1,3,2,0:T(8,128)S(1)}, f32[2,10,1,2,128]{4,1,3,2,0:T(8,128)S(1)}, u32[]{:S(2)}, u32[]{:S(2)}) collective-permute-start(f32[2,10,1,2,128]{4,1,3,2,0:T(8,128)S(1)} %get-tuple-element.183), channel_id=1, source_target_pairs={{0,2},{1,3},{4,6},{5,7},{8,10},{9,11},{12,14},{13,15},{16,18},{17,... | collective-permute-start | bytes 61448 | tf_op jit(solution)/shard_map/ppermute | solution.py:22
  40.9 7.3 %collective-permute-start.9 = (f32[2,10,1,2,128]{4,1,3,2,0:T(8,128)S(1)}, f32[2,10,1,2,128]{4,1,3,2,0:T(8,128)S(1)}, u32[]{:S(2)}, u32[]{:S(2)}) collective-permute-start(f32[2,10,1,2,128]{4,1,3,2,0:T(8,128)S(1)} %get-tuple-element.184), channel_id=1, source_target_pairs={{2,0},{3,1},{6,4},{7,5},{10,8},{11,9},{14,12},{15,13},{18,16},{19,... | collective-permute-start | bytes 61448 | tf_op jit(solution)/shard_map/ppermute | solution.py:25
  42.3 8.6 %collective-permute-start.2 = (f32[3,10,1,2,128]{4,3,2,1,0:T(2,128)S(1)}, f32[3,10,1,2,128]{4,3,2,1,0:T(2,128)S(1)}, u32[]{:S(2)}, u32[]{:S(2)}) collective-permute-start(f32[3,10,1,2,128]{4,3,2,1,0:T(2,128)S(1)} %get-tuple-element.185), channel_id=1, source_target_pairs={{0,2},{1,3},{4,6},{5,7},{8,10},{9,11},{12,14},{13,15},{16,18},{17,... | collective-permute-start | bytes 92168 | tf_op jit(solution)/shard_map/ppermute | solution.py:22
  46.9 5.8 %collective-permute-start.3 = (f32[3,10,1,2,128]{4,3,2,1,0:T(2,128)S(1)}, f32[3,10,1,2,128]{4,3,2,1,0:T(2,128)S(1)}, u32[]{:S(2)}, u32[]{:S(2)}) collective-permute-start(f32[3,10,1,2,128]{4,3,2,1,0:T(2,128)S(1)} %get-tuple-element.186), channel_id=1, source_target_pairs={{2,0},{3,1},{6,4},{7,5},{10,8},{11,9},{14,12},{15,13},{18,16},{19,... | collective-permute-start | bytes 92168 | tf_op jit(solution)/shard_map/ppermute | solution.py:25
  48.2 7.2 %collective-permute-start.10 = (f32[2,10,4,1,128]{4,1,3,2,0:T(8,128)S(1)}, f32[2,10,4,1,128]{4,1,3,2,0:T(8,128)S(1)}, u32[]{:S(2)}, u32[]{:S(2)}) collective-permute-start(f32[2,10,4,1,128]{4,1,3,2,0:T(8,128)S(1)} %get-tuple-element.177), channel_id=1, source_target_pairs={{0,1},{2,3},{4,5},{6,7},{8,9},{10,11},{12,13},{14,15},{16,17},{18,... | collective-permute-start | bytes 122888 | tf_op jit(solution)/shard_map/ppermute | solution.py:22
  49.6 5.8 %collective-permute-start.11 = (f32[2,10,4,1,128]{4,1,3,2,0:T(8,128)S(1)}, f32[2,10,4,1,128]{4,1,3,2,0:T(8,128)S(1)}, u32[]{:S(2)}, u32[]{:S(2)}) collective-permute-start(f32[2,10,4,1,128]{4,1,3,2,0:T(8,128)S(1)} %get-tuple-element.178), channel_id=1, source_target_pairs={{1,0},{3,2},{5,4},{7,6},{9,8},{11,10},{13,12},{15,14},{17,16},{19,... | collective-permute-start | bytes 122888 | tf_op jit(solution)/shard_map/ppermute | solution.py:25
  52.8 2.8 %collective-permute-start.4 = (f32[3,10,4,1,128]{4,3,2,1,0:T(1,128)S(1)}, f32[3,10,4,1,128]{4,3,2,1,0:T(1,128)S(1)}, u32[]{:S(2)}, u32[]{:S(2)}) collective-permute-start(f32[3,10,4,1,128]{4,3,2,1,0:T(1,128)S(1)} %get-tuple-element.179), channel_id=1, source_target_pairs={{0,1},{2,3},{4,5},{6,7},{8,9},{10,11},{12,13},{14,15},{16,17},{18,... | collective-permute-start | bytes 184328 | tf_op jit(solution)/shard_map/ppermute | solution.py:22
  54.1 3.1 %collective-permute-start.5 = (f32[3,10,4,1,128]{4,3,2,1,0:T(1,128)S(1)}, f32[3,10,4,1,128]{4,3,2,1,0:T(1,128)S(1)}, u32[]{:S(2)}, u32[]{:S(2)}) collective-permute-start(f32[3,10,4,1,128]{4,3,2,1,0:T(1,128)S(1)} %get-tuple-element.180), channel_id=1, source_target_pairs={{1,0},{3,2},{5,4},{7,6},{9,8},{11,10},{13,12},{15,14},{17,16},{19,... | collective-permute-start | bytes 184328 | tf_op jit(solution)/shard_map/ppermute | solution.py:25
  57.5 41.2 %copy-start.2 = (f32[3,8,2,2,128]{4,3,2,1,0:T(2,128)S(1)}, f32[3,8,2,2,128]{4,3,2,1,0:T(2,128)}, u32[]{:S(2)}) copy-start(f32[3,8,2,2,128]{4,3,2,1,0:T(2,128)} %param.16) | copy-start | bytes 147460
  57.5 47.1 %copy-start.5 = (s32[1,1,1,32,1]{3,4,2,1,0:T(1,128)S(1)}, s32[1,1,1,32,1]{3,4,2,1,0:T(1,128)}, u32[]{:S(2)}) copy-start(s32[1,1,1,32,1]{3,4,2,1,0:T(1,128)} %param.21) | copy-start | bytes 388
  98.8 6.0 %collective-permute-start.12 = (f32[3,1,2,2,128]{4,1,3,2,0:T(1,128)S(1)}, f32[3,1,2,2,128]{4,1,3,2,0:T(1,128)S(1)}, u32[]{:S(2)}, u32[]{:S(2)}) collective-permute-start(f32[3,1,2,2,128]{4,1,3,2,0:T(1,128)S(1)} %get-tuple-element.187), channel_id=1, source_target_pairs={{0,4},{4,8},{8,12},{1,5},{5,9},{9,13},{2,6},{6,10},{10,14},{3,7},{... | collective-permute-start | bytes 18440 | tf_op jit(solution)/shard_map/ppermute | solution.py:22
  103.3 5.5 %collective-permute-start.13 = (f32[3,1,2,2,128]{4,1,3,2,0:T(1,128)S(1)}, f32[3,1,2,2,128]{4,1,3,2,0:T(1,128)S(1)}, u32[]{:S(2)}, u32[]{:S(2)}) collective-permute-start(f32[3,1,2,2,128]{4,1,3,2,0:T(1,128)S(1)} %get-tuple-element.188), channel_id=1, source_target_pairs={{4,0},{8,4},{12,8},{5,1},{9,5},{13,9},{6,2},{10,6},{14,10},{7,3},{... | collective-permute-start | bytes 18440 | tf_op jit(solution)/shard_map/ppermute | solution.py:25
  108.9 6.2 %collective-permute-start.14 = (f32[3,10,1,2,128]{4,1,3,2,0:T(8,128)S(1)}, f32[3,10,1,2,128]{4,1,3,2,0:T(8,128)S(1)}, u32[]{:S(2)}, u32[]{:S(2)}) collective-permute-start(f32[3,10,1,2,128]{4,1,3,2,0:T(8,128)S(1)} %get-tuple-element.181), channel_id=1, source_target_pairs={{0,2},{1,3},{4,6},{5,7},{8,10},{9,11},{12,14},{13,15},{16,18},{17,... | collective-permute-start | bytes 92168 | tf_op jit(solution)/shard_map/ppermute | solution.py:22
  113.4 6.0 %collective-permute-start.15 = (f32[3,10,1,2,128]{4,1,3,2,0:T(8,128)S(1)}, f32[3,10,1,2,128]{4,1,3,2,0:T(8,128)S(1)}, u32[]{:S(2)}, u32[]{:S(2)}) collective-permute-start(f32[3,10,1,2,128]{4,1,3,2,0:T(8,128)S(1)} %get-tuple-element.182), channel_id=1, source_target_pairs={{2,0},{3,1},{6,4},{7,5},{10,8},{11,9},{14,12},{15,13},{18,16},{19,... | collective-permute-start | bytes 92168 | tf_op jit(solution)/shard_map/ppermute | solution.py:25
  119.4 2.6 %collective-permute-start.16 = (f32[3,10,4,1,128]{4,1,3,2,0:T(8,128)S(1)}, f32[3,10,4,1,128]{4,1,3,2,0:T(8,128)S(1)}, u32[]{:S(2)}, u32[]{:S(2)}) collective-permute-start(f32[3,10,4,1,128]{4,1,3,2,0:T(8,128)S(1)} %get-tuple-element.175), channel_id=1, source_target_pairs={{0,1},{2,3},{4,5},{6,7},{8,9},{10,11},{12,13},{14,15},{16,17},{18,... | collective-permute-start | bytes 184328 | tf_op jit(solution)/shard_map/ppermute | solution.py:22
  120.7 3.2 %collective-permute-start.17 = (f32[3,10,4,1,128]{4,1,3,2,0:T(8,128)S(1)}, f32[3,10,4,1,128]{4,1,3,2,0:T(8,128)S(1)}, u32[]{:S(2)}, u32[]{:S(2)}) collective-permute-start(f32[3,10,4,1,128]{4,1,3,2,0:T(8,128)S(1)} %get-tuple-element.176), channel_id=1, source_target_pairs={{1,0},{3,2},{5,4},{7,6},{9,8},{11,10},{13,12},{15,14},{17,16},{19,... | collective-permute-start | bytes 184328 | tf_op jit(solution)/shard_map/ppermute | solution.py:25
  124.2 41.4 %copy-start.4 = (s32[8,2,2,128]{3,2,1,0:T(2,128)S(1)}, s32[8,2,2,128]{3,2,1,0:T(2,128)}, u32[]{:S(2)}) copy-start(s32[8,2,2,128]{3,2,1,0:T(2,128)} %param.19) | copy-start | bytes 49156
  176.0 24.3 %copy-start.3 = (f32[3,256]{1,0:T(4,128)S(1)}, f32[3,256]{1,0:T(4,128)}, u32[]{:S(2)}) copy-start(f32[3,256]{1,0:T(4,128)} %param.20) | copy-start | bytes 9220
  178.4 22.5 %all-to-all-start = ((f32[8,64,128]{2,0,1:T(8,128)}), f32[8,64,128]{2,0,1:T(8,128)S(1)}, u32[]{:S(2)}, u32[]{:S(2)}) async-start(f32[8,64,128]{2,0,1:T(8,128)} %copy.106), calls=%async_computation | async-start | bytes 524288 | tf_op jit(solution)/shard_map/all_to_all | solution.py:109
Sparse Core Ops, SparseCore 0:
  177.2 20.9 reduce-scatter.3
where the time goes:
time: 210 us; the launch traced here: 209 us
  starting transfers between devices  45.9 us (22%)
  other arithmetic  41.2 us (20%)
  loops' own time  34.1 us (16%)
  waiting for transfers between devices  30 us (14%)
  local copies, waits for them, and re-layouts  22.7 us (11%)
  between operations  14.6 us (7%)
  matrix products  14.5 us (7%)
  blocking collectives  5.32 us (3%)
    another operation x2, loops' own time, contact_forces(): forces = lax.map(one_row, jnp.arange(rows, dtype=jnp.int32))  34.1 us
    ppermute x9, starting transfers between devices, padded_2(): lax.ppermute(lax.slice_in_dim(block, block.shape[dim] - width, None, axis...  30.4 us
    unnamed x2, waiting for transfers between devices  15.9 us
    reduce_sum x16, other arithmetic, one_row(): return -STIFF * jnp.sum(weight[None] * diff, axis=(1, 5))  13.6 us
    ppermute x9, waiting for transfers between devices, padded_2(): lax.ppermute(lax.slice_in_dim(block, 0, width, axis=dim), axis, backward)  13.6 us
    ppermute x9, starting transfers between devices, padded_2(): lax.ppermute(lax.slice_in_dim(block, 0, width, axis=dim), axis, backward)  11.6 us
    dynamic_slice x16, local copies, waits for them, and re-layouts, contact_forces(): forces = lax.map(one_row, jnp.arange(rows, dtype=jnp.int32))  10.4 us
    reduce_sum x16, other arithmetic, one_row(): dist = jnp.sum(diff * diff, axis=0)  9.87 us
  transfers between devices with their start and end apart: 20, of which 7 were waited for; matrix products, arithmetic and copies ran while one was open for 8% of the time, Pallas kernels for 0%

commit v1 on v0

v1 whole, which is shorter than its diff:
```python
import functools
import math

import jax
import jax.numpy as jnp
from jax import lax
from jax.experimental import pallas as pl
from jax.experimental.pallas import tpu as pltpu
from jax.sharding import PartitionSpec as P

STEP = 0.1
COUPLE = 0.5
RADIUS_REF = 0.45
SCALE = math.sqrt(math.log2(math.e))
PARK = 64.0
MESH = pl.DeviceIdType.MESH
F32 = jnp.float32
BF16 = jnp.bfloat16


def dot(a, b):
    return jnp.dot(a, b, preferred_element_type=F32)


def dot_t(a, b):
    return lax.dot_general(a, b, (((1,), (1,)), ((), ())), preferred_element_type=F32)


def split3(x):
    h = x.astype(BF16).astype(F32)
    rest = x - h
    m = rest.astype(BF16).astype(F32)
    return h, m, rest - m


def axis_sides(axis, n, size):
    me = lax.axis_index(axis)
    if n == 1:
        return []
    if n == 2:
        return [(1 - me, (size - 1) * (1 - me), size * (1 - me) - me, None)]
    return [(me - 1, 0, -1, me > 0), (me + 1, size - 1, size, me < n - 1)]


def maybe(cond, fn):
    if cond is None:
        fn()
    else:
        pl.when(cond)(fn)


def kernel(
    nl, nh, nw, dims,
    pos_ref, vel_ref, rad_ref, cnt_ref, cell_ref, flu_ref, plan_ref,
    moved_ref, fnext_ref,
    xr, vr, ur, accr, lv, xp, hl, hh, hw, lt, rr, qq, gg, tc, oh, ft, pb, pr,
    out0, out1, out2, in0, in1, in2,
    halo_send, halo_recv, grp_send, grp_recv, a2a_send, a2a_recv,
):
    gl, gh, gw, cap, spread = dims
    bins = gl * gh * gw
    layer = gh * gw
    groups = nh * nw
    me_l = lax.axis_index("len")
    me_h = lax.axis_index("ht")
    me_w = lax.axis_index("wd")
    me_g = me_h * nw + me_w

    barrier = pltpu.get_barrier_semaphore()

    def len_peer(k):
        return lax.rem(me_l + k, nl)

    def grp_peer(k):
        return lax.rem(me_g + k, groups)

    def grp_id(k):
        g = grp_peer(k)
        return {"ht": g // nw, "wd": lax.rem(g, nw)}

    for k in range(1, nl):
        pl.semaphore_signal(barrier, inc=1, device_id={"len": len_peer(k)}, device_id_type=MESH)
    for k in range(1, groups):
        pl.semaphore_signal(barrier, inc=1, device_id=grp_id(k), device_id_type=MESH)

    row = lax.broadcasted_iota(jnp.int32, (8, 128), 0)
    lane = lax.broadcasted_iota(jnp.int32, (1, 128), 1)

    def load_layer(l, _):
        for h in range(gh):
            for w in range(gw):
                b = l * layer + h * gw + w
                xr[b] = jnp.zeros((8, 128), F32)
                vr[b] = jnp.zeros((8, 128), F32)
                for c in range(3):
                    xr[b, c : c + 1, :] = pos_ref[c, l, h, w : w + 1, :]
                    vr[b, c : c + 1, :] = vel_ref[c, l, h, w : w + 1, :]
                xr[b, 3:4, :] = rad_ref[l, h, w : w + 1, :]
                live = lane < cnt_ref[l, h, w]
                lv[b] = jnp.broadcast_to(jnp.where(live, 1.0, 0.0), (8, 128))
                xp[0, l, h, w] = jnp.where((lv[b] > 0.5) | (row >= 3), xr[b], PARK)
        return 0

    lax.fori_loop(0, gl, load_layer, 0)
    for c in range(3):
        for s in range(spread):
            ft[0, c * spread + s : c * spread + s + 1, :] = flu_ref[c : c + 1, s * 128 : (s + 1) * 128]
    for r_ in range(3 * spread, 8):
        ft[0, r_ : r_ + 1, :] = jnp.zeros((1, 128), F32)

    plans = []
    for axis, n, size, ref in (("len", nl, gl, hl), ("ht", nh, gh, hh), ("wd", nw, gw, hw)):
        plans.append((axis, ref, axis_sides(axis, n, size)))
    empty = jnp.where(row < 3, PARK, RADIUS_REF)
    for axis, ref, sides in plans:
        for s, (partner, face, coord, exists) in enumerate(sides):
            if exists is not None:

                def fill(ref=ref, s=s):
                    for t in range(2):
                        ref[t, s] = jnp.broadcast_to(empty, ref.shape[2:])

                pl.when(jnp.logical_not(exists))(fill)

    pl.semaphore_wait(barrier, nl - 1 + groups - 1)

    def halo_copies(t):
        res = []
        for a, (axis, ref, sides) in enumerate(plans):
            for s, (partner, face, coord, exists) in enumerate(sides):
                back = s if len(sides) == 1 else 1 - s
                src = (xp.at[t, face], xp.at[t, :, face], xp.at[t, :, :, face])[a]
                send = pltpu.make_async_remote_copy(
                    src_ref=src, dst_ref=ref.at[t, back],
                    send_sem=halo_send.at[t, a, s], recv_sem=halo_recv.at[t, a, back],
                    device_id={axis: partner}, device_id_type=MESH,
                )
                recv = pltpu.make_async_remote_copy(
                    src_ref=src, dst_ref=ref.at[t, s],
                    send_sem=halo_send.at[t, a, s], recv_sem=halo_recv.at[t, a, s],
                    device_id={axis: partner}, device_id_type=MESH,
                )
                res.append((send, recv, exists))
        return res

    def start_halo(t):
        for send, recv, exists in halo_copies(t):
            maybe(exists, send.start)

    def wait_halo(t):
        for send, recv, exists in halo_copies(t):
            maybe(exists, recv.wait_recv)

    def wait_halo_sent(t):
        for send, recv, exists in halo_copies(t):
            maybe(exists, send.wait_send)

    def grp_copies(phase):
        res = []
        for k in range(1, groups):
            src = ft.at[0] if phase == 0 else pb.at[grp_peer(k)]
            dst = ft.at[k] if phase == 0 else pr.at[k - 1]
            res.append(pltpu.make_async_remote_copy(
                src_ref=src, dst_ref=dst, send_sem=grp_send.at[phase, k - 1],
                recv_sem=grp_recv.at[phase, k - 1], device_id=grp_id(k), device_id_type=MESH))
        return res

    def a2a_copies(phase):
        src, dst = ((out0, in0), (out1, in1), (out2, in2))[phase]
        res = []
        for k in range(1, nl):
            res.append(pltpu.make_async_remote_copy(
                src_ref=src.at[len_peer(k)], dst_ref=dst.at[k - 1], send_sem=a2a_send.at[phase, k - 1],
                recv_sem=a2a_recv.at[phase, k - 1], device_id={"len": len_peer(k)}, device_id_type=MESH))
        return res

    start_halo(0)
    for copy in grp_copies(0):
        copy.start()

    dest = plan_ref[...]
    marks = jnp.where(dest == lax.broadcasted_iota(jnp.int32, (16, bins), 0), 1.0, 0.0)
    before = jnp.where(
        lax.broadcasted_iota(jnp.int32, (bins, bins), 0) < lax.broadcasted_iota(jnp.int32, (bins, bins), 1),
        1.0, 0.0)
    earlier = dot(marks.astype(BF16), before.astype(BF16))
    rank = jnp.sum(earlier * marks, axis=0, keepdims=True)
    slot = dest * cap + rank.astype(jnp.int32)
    sel = jnp.where(slot == lax.broadcasted_iota(jnp.int32, (nl * cap, bins), 0), 1.0, 0.0)
    sel3 = jnp.concatenate([sel, sel, sel], axis=1).astype(BF16)

    def pack(values, out, c):
        parts = jnp.concatenate(split3(values), axis=0).astype(BF16)
        got = dot(sel3, parts)
        for d in range(nl):
            out[d, c] = got[d * cap : (d + 1) * cap]

    alive = lv[:, 0, :]
    pack(xr[:, 3, :] * alive, out0, 0)
    pack(alive, out0, 1)
    for copy in a2a_copies(0):
        copy.start()

    mid = ((gl - 1) / 2 + 0.5, gh / 2, gw / 2)

    def coords(tile, where):
        off = jnp.zeros((8, 128), F32)
        for c in range(3):
            off = jnp.where(row == c, jnp.asarray(where[c], F32) - mid[c], off)
        return jnp.where(row < 3, (tile + off) * SCALE, 0.0)

    def right_side(t, index, tile, place):
        norm = jnp.sum(place * place, axis=0, keepdims=True)
        h, m, l = split3(jnp.where(row < 3, 2.0 * place, jnp.where(row == 3, 1.0, jnp.where(row == 4, norm, 0.0))))
        zero = jnp.zeros((8, 128), F32)
        left = jnp.concatenate([h, m, h, m, l, h, zero, zero], axis=0)
        rr[index, :, 0:128] = left.astype(BF16)
        if t == 0:
            rh, rm, rl = split3(tile[3:4])
            reach = jnp.where(row < 3, 1.0, jnp.where(row == 3, rh, jnp.where(row == 4, rm, jnp.where(row == 5, rl, 0.0))))
            right = jnp.concatenate([zero] * 6 + [reach, zero], axis=0)
            rr[index, :, 128:256] = right.astype(BF16)
        h, m, l = split3(jnp.where(row == 3, 1.0, place))
        q = jnp.concatenate([h + pltpu.roll(m, 4, 0), l], axis=0)
        qq[index] = jnp.concatenate([q, q], axis=1).astype(BF16)

    def left_side(index, tile, place):
        norm = jnp.sum(place * place, axis=0, keepdims=True)
        h, m, l = split3(jnp.where(row < 3, place, jnp.where(row == 3, -norm, jnp.where(row == 4, -1.0, 0.0))))
        rh, rm, rl = split3(tile[3:4])
        reach = jnp.where(row == 0, rh, jnp.where(row == 1, rm, jnp.where(row == 2, rl, jnp.where(row < 6, 1.0, 0.0))))
        zero = jnp.zeros((8, 128), F32)
        full = jnp.concatenate([h, h, m, m, h, l, reach, zero], axis=0)
        lt[index] = full.T.astype(BF16)

    def pair(t, i, j, block):
        if t == 0:
            both = dot(lt[i], rr[j])
            dist = both[:, :128]
            inv = pl.reciprocal(both[:, 128:], approx=False)
            inv = inv * inv
            tc[block] = inv
        else:
            dist = dot(lt[i], rr[j, :, 0:128])
            inv = tc[block]
        e = jnp.exp2(dist * inv)
        high = e.astype(BF16)
        low = (e - high.astype(F32)).astype(BF16)
        return high, low

    def onto_j(i, e):
        return dot(qq[i], jnp.concatenate(e, axis=0))

    def onto_i(j, e):
        return dot_t(qq[j], jnp.concatenate(e, axis=1))

    ht_pairs = [(h * gw + w, (h + 1) * gw + w) for h in range(gh - 1) for w in range(gw)]
    wd_pairs = [(h * gw + w, h * gw + w + 1) for h in range(gh) for w in range(gw - 1)]
    in_layer = ht_pairs + wd_pairs
    per_layer = layer + len(in_layer)
    base_len = gl * per_layer
    base_halo = base_len + (gl - 1) * layer

    def prepare(t):
        def one(l, _):
            for h in range(gh):
                for w in range(gw):
                    b = l * layer + h * gw + w
                    tile = xp[t, l, h, w]
                    place = coords(tile, (l, h, w))
                    right_side(t, b, tile, place)
                    left_side(b, tile, place)
            return 0

        lax.fori_loop(0, gl, one, 0)

    def interior(t):
        def one(l, _):
            base = l * layer
            sums = [None] * layer
            for n_ in range(layer):
                sums[n_] = onto_j(base + n_, pair(t, base + n_, base + n_, l * per_layer + n_))
            for n_, (i, j) in enumerate(in_layer):
                e = pair(t, base + i, base + j, l * per_layer + layer + n_)
                sums[j] = sums[j] + onto_j(base + i, e)
                sums[i] = sums[i] + onto_i(base + j, e)
            for n_ in range(layer):
                gg[base + n_] = sums[n_]
            return 0

        lax.fori_loop(0, gl, one, 0)

        def along(l, _):
            base = l * layer
            ups, downs = [], []
            for n_ in range(layer):
                e = pair(t, base + n_, base + layer + n_, base_len + base + n_)
                ups.append(onto_j(base + n_, e))
                downs.append(onto_i(base + layer + n_, e))
            for n_ in range(layer):
                gg[base + n_] += downs[n_]
                gg[base + layer + n_] += ups[n_]
            return 0

        lax.fori_loop(0, gl - 1, along, 0)

    def boundary(t):
        at = bins
        for s, (partner, face, coord, exists) in enumerate(plans[0][2]):
            sums = []
            for h in range(gh):
                for w in range(gw):
                    tile = hl[t, s, h, w]
                    right_side(t, at + h * gw + w, tile, coords(tile, (coord, h, w)))
            for n_ in range(layer):
                e = pair(t, face * layer + n_, at + n_, base_halo + at - bins + n_)
                sums.append(onto_i(at + n_, e))
            for n_ in range(layer):
                gg[face * layer + n_] += sums[n_]
            at += layer
        for a, across in ((1, gw), (2, gh)):
            ref = plans[a][1]
            for s, (partner, face, coord, exists) in enumerate(plans[a][2]):

                def one(l, _, ref=ref, s=s, face=face, coord=coord, a=a, across=across, at=at):
                    targets, sums = [], []
                    for y in range(across):
                        tile = ref[t, s, l, y]
                        place = coords(tile, (l, coord, y) if a == 1 else (l, y, coord))
                        right_side(t, at + l * across + y, tile, place)
                    for y in range(across):
                        n_ = at + l * across + y
                        target = l * layer + (face * gw + y if a == 1 else y * gw + face)
                        e = pair(t, target, n_, base_halo + n_ - bins)
                        targets.append(target)
                        sums.append(onto_i(n_, e))
                    for target, got in zip(targets, sums):
                        gg[target] += got
                    return 0

                lax.fori_loop(0, gl, one, 0)
                at += gl * across

    lo_rows = lax.broadcasted_iota(jnp.int32, (128, 128), 0)

    def hi_mask(cells, g):
        return lax.shift_right_logical(cells, 7) == g * spread + lax.rem(row, spread)

    def read_fluid():
        for copy in grp_copies(0):
            copy.wait_recv()
        table = []
        for k in range(groups):
            table.append(ft[k])
        table = jnp.concatenate(table, axis=0)
        table = jnp.concatenate(split3(table), axis=0).astype(BF16)

        def one(l, _):
            for h in range(gh):
                for w in range(gw):
                    n_ = h * gw + w
                    cells = cell_ref[l, h, w : w + 1, :]
                    low = lax.rem(cells, 128)
                    oh[l, :, n_ * 128 : (n_ + 1) * 128] = jnp.where(low == lo_rows, 1.0, 0.0).astype(BF16)
            got = dot(table, oh[l])
            full = got[: groups * 8] + got[groups * 8 : groups * 16] + got[groups * 16 :]
            for h in range(gh):
                for w in range(gw):
                    n_ = h * gw + w
                    cells = cell_ref[l, h, w : w + 1, :]
                    mine = full[:, n_ * 128 : (n_ + 1) * 128]
                    u = jnp.zeros((8, 128), F32)
                    for k in range(groups):
                        g = lax.rem(me_g - k + groups, groups)
                        u = u + jnp.where(hi_mask(cells, g), mine[k * 8 : (k + 1) * 8], 0.0)
                    b = l * layer + n_
                    ur[b] = jnp.zeros((8, 128), F32)
                    for c in range(3):
                        ur[b, c : c + 1, :] = jnp.sum(u[c * spread : (c + 1) * spread], axis=0, keepdims=True)
            return 0

        lax.fori_loop(0, gl, one, 0)

    def update(t):
        def one(l, _):
            for h in range(gh):
                for w in range(gw):
                    b = l * layer + h * gw + w
                    tile = xr[b]
                    radius = tile[3:4]
                    ratio = radius * (1.0 / RADIUS_REF)
                    mass = ratio * ratio * ratio
                    place = coords(xp[t, l, h, w], (l, h, w))
                    g = gg[b]
                    total = g[:8] + pltpu.roll(g[:8], 4, 0) + g[8:]
                    force = (place * total[3:4] - total) * (1.0 / SCALE)
                    speed = vr[b]
                    drag = radius * (ur[b] - speed)
                    accr[b] = drag if t == 0 else accr[b] + drag
                    speed = speed + STEP * (force + drag) * (1.0 / mass)
                    alive = lv[b] > 0.5
                    speed = jnp.where((row < 3) & alive, speed, 0.0)
                    vr[b] = speed
                    if t == 0:
                        tile = tile + STEP * speed
                        xr[b] = tile
                        xp[1, l, h, w] = jnp.where(alive | (row >= 3), tile, PARK)
            return 0

        lax.fori_loop(0, gl, one, 0)

    prepare(0)
    interior(0)
    read_fluid()
    wait_halo(0)
    boundary(0)
    update(0)
    start_halo(1)
    for c in range(3):
        pack(xr[:, c, :] * alive, out1, c)
    for copy in a2a_copies(1):
        copy.start()

    prepare(1)
    interior(1)
    wait_halo(1)
    boundary(1)
    update(1)
    for c in range(3):
        pack(vr[:, c, :], out2, c)
    for copy in a2a_copies(2):
        copy.start()

    def cell_sums(l, total):
        lefts = []
        for h in range(gh):
            for w in range(gw):
                b = l * layer + h * gw + w
                cells = cell_ref[l, h, w : w + 1, :]
                radius = xr[b, 3:4, :]
                ratio = radius * (1.0 / RADIUS_REF)
                live_row = lv[b, 0:1, :]
                rows = [accr[b, c : c + 1, :] * live_row for c in range(3)] + [ratio * ratio * ratio * live_row]
                term = jnp.concatenate([rows[r_ // spread] for r_ in range(4 * spread)], axis=0)
                parts = split3(term)
                pieces = []
                for part in parts:
                    for g in range(groups):
                        pieces.append(jnp.where(hi_mask(cells, g), part, 0.0))
                lefts.append(jnp.concatenate(pieces, axis=0).astype(BF16))
        return total + dot_t(jnp.concatenate(lefts, axis=1), oh[l])

    sums = lax.fori_loop(0, gl, cell_sums, jnp.zeros((groups * 24, 128), F32))
    sums = sums[: groups * 8] + sums[groups * 8 : groups * 16] + sums[groups * 16 :]
    for g in range(groups):
        pb[g] = sums[g * 8 : (g + 1) * 8]
    for copy in grp_copies(1):
        copy.start()

    def landed(own, arrived, c, put):
        put(me_l, own[me_l, c])
        for k in range(1, nl):
            put(lax.rem(me_l - k + nl, nl), arrived[k - 1, c])

    for copy in a2a_copies(0) + a2a_copies(1):
        copy.wait_recv()
    for k in range(nl):
        source = lax.rem(me_l - k + nl, nl)
        at = pl.ds(source * cap, cap)
        early = out0.at[me_l] if k == 0 else in0.at[k - 1]
        for c in range(2):
            moved_ref[6 + c, at, :] = early[c]

    for copy in grp_copies(1):
        copy.wait_recv()
    whole = pb[me_g]
    for k in range(groups - 1):
        whole = whole + pr[k]
    mass_rows = whole[3 * spread : 4 * spread]
    for c in range(3):
        ratio = whole[c * spread : (c + 1) * spread] / (1.0 + mass_rows)
        fresh = ft[0, c * spread : (c + 1) * spread, :] - COUPLE * ratio
        for s in range(spread):
            fnext_ref[c : c + 1, s * 128 : (s + 1) * 128] = fresh[s : s + 1]

    for copy in a2a_copies(2):
        copy.wait_recv()
    for k in range(nl):
        source = lax.rem(me_l - k + nl, nl)
        at = pl.ds(source * cap, cap)
        place = out1.at[me_l] if k == 0 else in1.at[k - 1]
        speed = out2.at[me_l] if k == 0 else in2.at[k - 1]
        for c in range(3):
            v = speed[c]
            moved_ref[3 + c, at, :] = v
            moved_ref[c, at, :] = place[c] + STEP * v

    for t in range(2):
        wait_halo_sent(t)
        for copy in grp_copies(t):
            copy.wait_send()
    for phase in range(3):
        for copy in a2a_copies(phase):
            copy.wait_send()


def per_device(nl, nh, nw, positions, velocities, radius, counts, cell_index, fluid_velocity, plan):
    gl, gh, gw, slots = radius.shape
    bins = gl * gh * gw
    cap = max(2, 2 * bins // nl)
    spread = fluid_velocity.shape[1] // 128
    groups = nh * nw
    dims = (gl, gh, gw, cap, spread)

    def count(n):
        return 1 if n <= 2 else 2

    sl, sh, sw = count(nl), count(nh), count(nw)
    halos = sl * gh * gw + sh * gl * gw + sw * gl * gh
    blocks = gl * (gh * gw + (gh - 1) * gw + gh * (gw - 1)) + (gl - 1) * gh * gw + halos
    vmem = pltpu.VMEM
    scratch = [
        vmem((bins, 8, 128), F32), vmem((bins, 8, 128), F32), vmem((bins, 8, 128), F32),
        vmem((bins, 8, 128), F32), vmem((bins, 8, 128), F32),
        vmem((2, gl, gh, gw, 8, 128), F32),
        vmem((2, sl, gh, gw, 8, 128), F32), vmem((2, sh, gl, gw, 8, 128), F32), vmem((2, sw, gl, gh, 8, 128), F32),
        vmem((bins, 128, 64), BF16), vmem((bins + halos, 64, 256), BF16), vmem((bins + halos, 16, 256), BF16),
        vmem((bins, 16, 128), F32), vmem((blocks, 128, 128), F32),
        vmem((gl, 128, gh * gw * 128), BF16),
        vmem((groups, 8, 128), F32), vmem((groups, 8, 128), F32), vmem((max(1, groups - 1), 8, 128), F32),
        vmem((nl, 2, cap, 128), F32), vmem((nl, 3, cap, 128), F32), vmem((nl, 3, cap, 128), F32),
        vmem((nl - 1, 2, cap, 128), F32), vmem((nl - 1, 3, cap, 128), F32), vmem((nl - 1, 3, cap, 128), F32),
        pltpu.SemaphoreType.DMA((2, 3, 2)), pltpu.SemaphoreType.DMA((2, 3, 2)),
        pltpu.SemaphoreType.DMA((2, groups)), pltpu.SemaphoreType.DMA((2, groups)),
        pltpu.SemaphoreType.DMA((3, nl)), pltpu.SemaphoreType.DMA((3, nl)),
    ]
    in_vmem = pl.BlockSpec(memory_space=pltpu.VMEM)
    in_smem = pl.BlockSpec(memory_space=pltpu.SMEM)
    moved, fluid_next = pl.pallas_call(
        functools.partial(kernel, nl, nh, nw, dims),
        out_shape=(
            jax.ShapeDtypeStruct((8, nl * cap, slots), F32),
            jax.ShapeDtypeStruct(fluid_velocity.shape, F32),
        ),
        in_specs=[in_vmem, in_vmem, in_vmem, in_smem, in_vmem, in_vmem, in_vmem],
        out_specs=(in_vmem, in_vmem),
        scratch_shapes=scratch,
        compiler_params=pltpu.CompilerParams(
            collective_id=0, has_side_effects=True, vmem_limit_bytes=48 * 1024 * 1024
        ),
    )(positions, velocities, radius, counts, cell_index, fluid_velocity, plan.reshape(1, bins))
    return moved.reshape(8, 1, 1, nl * cap, slots), fluid_next


def solution(mesh):
    sizes = dict(mesh.shape)
    in_specs = (
        P(None, ("section", "len"), "ht", "wd", None),
        P(None, ("section", "len"), "ht", "wd", None),
        P(("section", "len"), "ht", "wd", None),
        P(("section", "len"), "ht", "wd"),
        P(("section", "len"), "ht", "wd", None),
        P(None, ("section", "len", "ht", "wd")),
        P(("section", "len"), "ht", "wd", None, None),
    )
    out_specs = (
        P(None, "ht", "wd", ("section", "len"), None),
        P(None, ("section", "len", "ht", "wd")),
    )
    body = functools.partial(per_device, sizes["len"], sizes["ht"], sizes["wd"])
    return jax.shard_map(body, mesh=mesh, in_specs=in_specs, out_specs=out_specs, check_vma=False)
```

time: 210 us -> 57.4 us (0.27)
  Pallas kernels: 0 us -> 51.3 us
  starting transfers between devices: 45.9 us -> 0 us
  other arithmetic: 41.2 us -> 0 us
  loops' own time: 34.1 us -> 0 us
  waiting for transfers between devices: 30 us -> 0 us
  local copies, waits for them, and re-layouts: 22.7 us -> 5.12 us
  matrix products: 14.5 us -> 0 us
  between operations: 14.6 us -> 0.66 us
  blocking collectives: 5.32 us -> 0 us
    pallas_call x0 -> x1, Pallas kernels: none -> 51.3 us  [per_device(): pl.pallas_call(functools.partial(kernel, nl, nh, nw, dims), out_shape=(ja...]
    ppermute x18 -> x0, starting transfers between devices: 42 us -> none  [the longest x9 30.4 us: padded_2(): lax.ppermute(lax.slice_in_dim(block, block.shape[dim] - width, None, axis...]
    another operation x3 -> x0, loops' own time: 34.1 us -> none  [the longest x2 34.1 us: contact_forces(): forces = lax.map(one_row, jnp.arange(rows, dtype=jnp.int32))]
    reduce_sum x33 -> x0, other arithmetic: 23.6 us -> none  [the longest x16 13.6 us: one_row(): return -STIFF * jnp.sum(weight[None] * diff, axis=(1, 5))]
    unnamed x2 -> x0, waiting for transfers between devices: 15.9 us -> none
    dot_general x6 -> x0, matrix products: 14.5 us -> none  [the longest x1 8.72 us: per_device(): fluid_here = jnp.einsum('cf,pf->cp', piece, onehot, precision=HIGHEST)]
    ppermute x18 -> x0, waiting for transfers between devices: 14 us -> none  [the longest x9 13.6 us: padded_2(): lax.ppermute(lax.slice_in_dim(block, 0, width, axis=dim), axis, backward)]
    dynamic_slice x20 -> x0, local copies, waits for them, and re-layouts: 12.7 us -> none  [the longest x16 10.4 us: contact_forces(): forces = lax.map(one_row, jnp.arange(rows, dtype=jnp.int32))]
  transfers between devices with their start and end apart: 20 -> 0, of which waited for: 7 -> 0; matrix products, arithmetic and copies ran while one was open for 8% -> 0% of each run, Pallas kernels for 0% -> 0%
where the time goes in v1:
time: 57.4 us; the launch traced here: 57 us
  Pallas kernels  51.3 us (89%)
  local copies, waits for them, and re-layouts  5.12 us (9%)
  between operations  0.66 us (1%)
    pallas_call x1, Pallas kernels, per_device(): pl.pallas_call(functools.partial(kernel, nl, nh, nw, dims), out_shape=(ja...  51.3 us
    unnamed x15, local copies, waits for them, and re-layouts  5.12 us

profile of v1, /device:TPU:0, one launch (start us, length us, event | category | flops | bytes accessed | tf_op | source)
XLA Modules:
  0.0 57.0 jit_solution(16398283950192208701)
XLA Ops:
  0.6 0.0 copy-start.4
  0.6 0.0 copy-start.5
  0.7 0.8 %copy.9.cnt_ref = s32[8,2,2]{2,1,0:T(2,128)S(1)} copy(s32[8,2,2]{0,2,1:T(2,128)} %param.10) | data formatting | bytes 256 | tf_op args[3]
  1.4 0.0 copy-done.4
  1.4 0.0 copy-done.5
  1.4 0.0 copy-start
  1.4 0.8 %copy-done = f32[3,8,2,2,128]{4,3,2,1,0:T(2,128)S(1)} copy-done((f32[3,8,2,2,128]{4,3,2,1,0:T(2,128)S(1)}, f32[3,8,2,2,128]{4,3,2,1,0:T(2,128)}, u32[]{:S(2)}) %copy-start) | copy-done | bytes 49176
  2.2 0.0 copy-start.1
  2.2 0.8 %copy-done.1 = f32[3,8,2,2,128]{4,3,2,1,0:T(2,128)S(1)} copy-done((f32[3,8,2,2,128]{4,3,2,1,0:T(2,128)S(1)}, f32[3,8,2,2,128]{4,3,2,1,0:T(2,128)}, u32[]{:S(2)}) %copy-start.1) | copy-done | bytes 49176
  3.0 0.0 copy-start.2
  3.0 0.7 %copy-done.2 = f32[8,2,2,128]{3,2,1,0:T(2,128)S(1)} copy-done((f32[8,2,2,128]{3,2,1,0:T(2,128)S(1)}, f32[8,2,2,128]{3,2,1,0:T(2,128)}, u32[]{:S(2)}) %copy-start.2) | copy-done | bytes 16408
  3.8 0.0 copy-start.3
  3.8 0.7 %copy-done.3 = s32[8,2,2,128]{3,2,1,0:T(2,128)S(1)} copy-done((s32[8,2,2,128]{3,2,1,0:T(2,128)S(1)}, s32[8,2,2,128]{3,2,1,0:T(2,128)}, u32[]{:S(2)}) %copy-start.3) | copy-done | bytes 16408
  4.5 51.3 %shard_map.86 = (f32[8,64,128]{2,1,0:T(8,128)S(1)}, f32[3,256]{1,0:T(4,128)S(1)}) custom-call(f32[3,8,2,2,128]{4,3,2,1,0:T(2,128)S(1)} %copy-done, f32[3,8,2,2,128]{4,3,2,1,0:T(2,128)S(1)} %copy-done.1, f32[8,2,2,128]{3,2,1,0:T(2,128)S(1)} %copy-done.2, s32[8,2,2]{2,1,0:T(2,128)S(1)} %copy.9.cnt_ref, s32[8,2,2,128]{3,2,1,0:T(2,128)S(1)} %copy-done.3, ...), custom_call_target="tpu_custom_call" | custom-call | tf_op jit(solution)/shard_map/pallas_call | solution.py:539
  55.8 0.7 %copy.13 = f32[8,1,1,64,128]{4,3,2,1,0:T(8,128)} copy(f32[8,1,1,64,128]{4,3,2,1,0:T(8,128)S(1)} %bitcast.4) | data formatting | bytes 524288
  56.5 0.6 %copy.14 = f32[3,256]{1,0:T(4,128)} copy(f32[3,256]{1,0:T(4,128)S(1)} %get-tuple-element.11) | data formatting | bytes 6144
Async XLA Ops:
  0.6 0.8 %copy-start.4 = (f32[3,256]{1,0:T(4,128)S(1)}, f32[3,256]{1,0:T(4,128)}, u32[]{:S(2)}) copy-start(f32[3,256]{1,0:T(4,128)} %flu_ref.1) | copy-start | bytes 9220
  0.6 0.8 %copy-start.5 = (s32[1,1,1,32,1]{3,4,2,1,0:T(1,128)S(1)}, s32[1,1,1,32,1]{3,4,2,1,0:T(1,128)}, u32[]{:S(2)}) copy-start(s32[1,1,1,32,1]{3,4,2,1,0:T(1,128)} %param.13) | copy-start | bytes 388
  1.4 0.8 %copy-start = (f32[3,8,2,2,128]{4,3,2,1,0:T(2,128)S(1)}, f32[3,8,2,2,128]{4,3,2,1,0:T(2,128)}, u32[]{:S(2)}) copy-start(f32[3,8,2,2,128]{4,3,2,1,0:T(2,128)} %pos_ref.1) | copy-start | bytes 147460
  2.2 0.8 %copy-start.1 = (f32[3,8,2,2,128]{4,3,2,1,0:T(2,128)S(1)}, f32[3,8,2,2,128]{4,3,2,1,0:T(2,128)}, u32[]{:S(2)}) copy-start(f32[3,8,2,2,128]{4,3,2,1,0:T(2,128)} %vel_ref.1) | copy-start | bytes 147460
  3.0 0.7 %copy-start.2 = (f32[8,2,2,128]{3,2,1,0:T(2,128)S(1)}, f32[8,2,2,128]{3,2,1,0:T(2,128)}, u32[]{:S(2)}) copy-start(f32[8,2,2,128]{3,2,1,0:T(2,128)} %rad_ref.1) | copy-start | bytes 49156
  3.8 0.7 %copy-start.3 = (s32[8,2,2,128]{3,2,1,0:T(2,128)S(1)}, s32[8,2,2,128]{3,2,1,0:T(2,128)}, u32[]{:S(2)}) copy-start(s32[8,2,2,128]{3,2,1,0:T(2,128)} %cell_ref.1) | copy-start | bytes 49156

commit v2 on v1

--- a/solution.py
+++ b/solution.py
@@ -1,5 +1,4 @@
 import functools
-import math
 
 import jax
 import jax.numpy as jnp
@@ -11,7 +10,6 @@
 STEP = 0.1
 COUPLE = 0.5
 RADIUS_REF = 0.45
-SCALE = math.sqrt(math.log2(math.e))
 PARK = 64.0
 MESH = pl.DeviceIdType.MESH
 F32 = jnp.float32
@@ -53,7 +51,7 @@
     nl, nh, nw, dims,
     pos_ref, vel_ref, rad_ref, cnt_ref, cell_ref, flu_ref, plan_ref,
     moved_ref, fnext_ref,
-    xr, vr, ur, accr, lv, xp, hl, hh, hw, lt, rr, qq, gg, tc, oh, ft, pb, pr,
+    xr, vr, ur, accr, lv, xp, hl, hh, hw, lt, rr, pc, gg, tc, oh, ft, pb, pr,
     out0, out1, out2, in0, in1, in2,
     halo_send, halo_recv, grp_send, grp_recv, a2a_send, a2a_recv,
 ):
@@ -207,12 +205,19 @@
         off = jnp.zeros((8, 128), F32)
         for c in range(3):
             off = jnp.where(row == c, jnp.asarray(where[c], F32) - mid[c], off)
-        return jnp.where(row < 3, (tile + off) * SCALE, 0.0)
+        return jnp.where(row < 3, tile + off, 0.0)
+
+    zero = jnp.zeros((8, 128), F32)
+    part_row = lax.broadcasted_iota(jnp.int32, (64, 384), 0)
+    part_of = part_row // 8
+    spread_out = jnp.where(
+        (lax.rem(part_row, 8) == lax.broadcasted_iota(jnp.int32, (64, 384), 1) // 128)
+        & ((part_of == 0) | (part_of == 2) | (part_of == 5)),
+        1.0, 0.0).astype(BF16)
 
     def right_side(t, index, tile, place):
         norm = jnp.sum(place * place, axis=0, keepdims=True)
         h, m, l = split3(jnp.where(row < 3, 2.0 * place, jnp.where(row == 3, 1.0, jnp.where(row == 4, norm, 0.0))))
-        zero = jnp.zeros((8, 128), F32)
         left = jnp.concatenate([h, m, h, m, l, h, zero, zero], axis=0)
         rr[index, :, 0:128] = left.astype(BF16)
         if t == 0:
@@ -220,46 +225,45 @@
             reach = jnp.where(row < 3, 1.0, jnp.where(row == 3, rh, jnp.where(row == 4, rm, jnp.where(row == 5, rl, 0.0))))
             right = jnp.concatenate([zero] * 6 + [reach, zero], axis=0)
             rr[index, :, 128:256] = right.astype(BF16)
-        h, m, l = split3(jnp.where(row == 3, 1.0, place))
-        q = jnp.concatenate([h + pltpu.roll(m, 4, 0), l], axis=0)
-        qq[index] = jnp.concatenate([q, q], axis=1).astype(BF16)
 
     def left_side(index, tile, place):
         norm = jnp.sum(place * place, axis=0, keepdims=True)
         h, m, l = split3(jnp.where(row < 3, place, jnp.where(row == 3, -norm, jnp.where(row == 4, -1.0, 0.0))))
         rh, rm, rl = split3(tile[3:4])
         reach = jnp.where(row == 0, rh, jnp.where(row == 1, rm, jnp.where(row == 2, rl, jnp.where(row < 6, 1.0, 0.0))))
-        zero = jnp.zeros((8, 128), F32)
         full = jnp.concatenate([h, h, m, m, h, l, reach, zero], axis=0)
-        lt[index] = full.T.astype(BF16)
-
-    def pair(t, i, j, block):
+        left = full.T.astype(BF16)
+        lt[index] = left
+        pc[index] = dot(left, spread_out)
+
+    def push(t, target, source, block):
         if t == 0:
-            both = dot(lt[i], rr[j])
+            both = dot(lt[source], rr[target])
             dist = both[:, :128]
             inv = pl.reciprocal(both[:, 128:], approx=False)
             inv = inv * inv
             tc[block] = inv
         else:
-            dist = dot(lt[i], rr[j, :, 0:128])
+            dist = dot(lt[source], rr[target, :, 0:128])
             inv = tc[block]
-        e = jnp.exp2(dist * inv)
-        high = e.astype(BF16)
-        low = (e - high.astype(F32)).astype(BF16)
-        return high, low
-
-    def onto_j(i, e):
-        return dot(qq[i], jnp.concatenate(e, axis=0))
-
-    def onto_i(j, e):
-        return dot_t(qq[j], jnp.concatenate(e, axis=1))
-
-    ht_pairs = [(h * gw + w, (h + 1) * gw + w) for h in range(gh - 1) for w in range(gw)]
-    wd_pairs = [(h * gw + w, h * gw + w + 1) for h in range(gh) for w in range(gw - 1)]
-    in_layer = ht_pairs + wd_pairs
-    per_layer = layer + len(in_layer)
+        e = jnp.exp(dist * inv)
+        acc = [None] * 4
+        for k in range(16):
+            piece = e[8 * k : 8 * k + 8]
+            terms = [piece * pc[source, 8 * k : 8 * k + 8, 128 * c : 128 * c + 128] for c in range(3)] + [piece]
+            acc = terms if k == 0 else [a + b for a, b in zip(acc, terms)]
+        return jnp.concatenate(acc, axis=0)
+
+    near = []
+    for h in range(gh):
+        for w in range(gw):
+            near.append((h * gw + w, h * gw + w))
+            for h2, w2 in ((h - 1, w), (h + 1, w), (h, w - 1), (h, w + 1)):
+                if 0 <= h2 < gh and 0 <= w2 < gw:
+                    near.append((h * gw + w, h2 * gw + w2))
+    per_layer = len(near)
     base_len = gl * per_layer
-    base_halo = base_len + (gl - 1) * layer
+    base_halo = base_len + 2 * (gl - 1) * layer
 
     def prepare(t):
         def one(l, _):
@@ -278,12 +282,9 @@
         def one(l, _):
             base = l * layer
             sums = [None] * layer
-            for n_ in range(layer):
-                sums[n_] = onto_j(base + n_, pair(t, base + n_, base + n_, l * per_layer + n_))
-            for n_, (i, j) in enumerate(in_layer):
-                e = pair(t, base + i, base + j, l * per_layer + layer + n_)
-                sums[j] = sums[j] + onto_j(base + i, e)
-                sums[i] = sums[i] + onto_i(base + j, e)
+            for n_, (i, j) in enumerate(near):
+                got = push(t, base + i, base + j, l * per_layer + n_)
+                sums[i] = got if sums[i] is None else sums[i] + got
             for n_ in range(layer):
                 gg[base + n_] = sums[n_]
             return 0
@@ -294,9 +295,9 @@
             base = l * layer
             ups, downs = [], []
             for n_ in range(layer):
-                e = pair(t, base + n_, base + layer + n_, base_len + base + n_)
-                ups.append(onto_j(base + n_, e))
-                downs.append(onto_i(base + layer + n_, e))
+                block = base_len + 2 * (base + n_)
+                ups.append(push(t, base + layer + n_, base + n_, block))
+                downs.append(push(t, base + n_, base + layer + n_, block + 1))
             for n_ in range(layer):
                 gg[base + n_] += downs[n_]
                 gg[base + layer + n_] += ups[n_]
@@ -311,34 +312,37 @@
             for h in range(gh):
                 for w in range(gw):
                     tile = hl[t, s, h, w]
-                    right_side(t, at + h * gw + w, tile, coords(tile, (coord, h, w)))
+                    left_side(at + h * gw + w, tile, coords(tile, (coord, h, w)))
             for n_ in range(layer):
-                e = pair(t, face * layer + n_, at + n_, base_halo + at - bins + n_)
-                sums.append(onto_i(at + n_, e))
+                sums.append(push(t, face * layer + n_, at + n_, base_halo + at - bins + n_))
             for n_ in range(layer):
                 gg[face * layer + n_] += sums[n_]
             at += layer
         for a, across in ((1, gw), (2, gh)):
             ref = plans[a][1]
             for s, (partner, face, coord, exists) in enumerate(plans[a][2]):
-
-                def one(l, _, ref=ref, s=s, face=face, coord=coord, a=a, across=across, at=at):
+                step = 2 if gl % 2 == 0 else 1
+
+                def one(p, _, ref=ref, s=s, face=face, coord=coord, a=a, across=across, at=at, step=step):
                     targets, sums = [], []
-                    for y in range(across):
-                        tile = ref[t, s, l, y]
-                        place = coords(tile, (l, coord, y) if a == 1 else (l, y, coord))
-                        right_side(t, at + l * across + y, tile, place)
-                    for y in range(across):
-                        n_ = at + l * across + y
-                        target = l * layer + (face * gw + y if a == 1 else y * gw + face)
-                        e = pair(t, target, n_, base_halo + n_ - bins)
-                        targets.append(target)
-                        sums.append(onto_i(n_, e))
+                    for q in range(step):
+                        l = p * step + q
+                        for y in range(across):
+                            tile = ref[t, s, l, y]
+                            place = coords(tile, (l, coord, y) if a == 1 else (l, y, coord))
+                            left_side(at + l * across + y, tile, place)
+                    for q in range(step):
+                        l = p * step + q
+                        for y in range(across):
+                            n_ = at + l * across + y
+                            target = l * layer + (face * gw + y if a == 1 else y * gw + face)
+                            targets.append(target)
+                            sums.append(push(t, target, n_, base_halo + n_ - bins))
                     for target, got in zip(targets, sums):
                         gg[target] += got
                     return 0
 
-                lax.fori_loop(0, gl, one, 0)
+                lax.fori_loop(0, gl // step, one, 0)
                 at += gl * across
 
     lo_rows = lax.broadcasted_iota(jnp.int32, (128, 128), 0)
@@ -392,8 +396,9 @@
                     mass = ratio * ratio * ratio
                     place = coords(xp[t, l, h, w], (l, h, w))
                     g = gg[b]
-                    total = g[:8] + pltpu.roll(g[:8], 4, 0) + g[8:]
-                    force = (place * total[3:4] - total) * (1.0 / SCALE)
+                    rows = [jnp.sum(g[8 * c : 8 * c + 8], axis=0, keepdims=True) for c in range(4)]
+                    total = jnp.concatenate(rows + rows, axis=0)
+                    force = place * rows[3] - total
                     speed = vr[b]
                     drag = radius * (ur[b] - speed)
                     accr[b] = drag if t == 0 else accr[b] + drag
@@ -517,15 +522,15 @@
 
     sl, sh, sw = count(nl), count(nh), count(nw)
     halos = sl * gh * gw + sh * gl * gw + sw * gl * gh
-    blocks = gl * (gh * gw + (gh - 1) * gw + gh * (gw - 1)) + (gl - 1) * gh * gw + halos
+    blocks = gl * (gh * gw + 2 * (gh - 1) * gw + 2 * gh * (gw - 1)) + 2 * (gl - 1) * gh * gw + halos
     vmem = pltpu.VMEM
     scratch = [
         vmem((bins, 8, 128), F32), vmem((bins, 8, 128), F32), vmem((bins, 8, 128), F32),
         vmem((bins, 8, 128), F32), vmem((bins, 8, 128), F32),
         vmem((2, gl, gh, gw, 8, 128), F32),
         vmem((2, sl, gh, gw, 8, 128), F32), vmem((2, sh, gl, gw, 8, 128), F32), vmem((2, sw, gl, gh, 8, 128), F32),
-        vmem((bins, 128, 64), BF16), vmem((bins + halos, 64, 256), BF16), vmem((bins + halos, 16, 256), BF16),
-        vmem((bins, 16, 128), F32), vmem((blocks, 128, 128), F32),
+        vmem((bins + halos, 128, 64), BF16), vmem((bins, 64, 256), BF16), vmem((bins + halos, 128, 384), F32),
+        vmem((bins, 32, 128), F32), vmem((blocks, 128, 128), F32),
         vmem((gl, 128, gh * gw * 128), BF16),
         vmem((groups, 8, 128), F32), vmem((groups, 8, 128), F32), vmem((max(1, groups - 1), 8, 128), F32),
         vmem((nl, 2, cap, 128), F32), vmem((nl, 3, cap, 128), F32), vmem((nl, 3, cap, 128), F32),

time: 57.4 us -> 47.6 us (0.83)
  Pallas kernels: 51.3 us -> 41.5 us
    pallas_call x1, Pallas kernels: 51.3 us -> 41.5 us  [per_device(): pl.pallas_call(functools.partial(kernel, nl, nh, nw, dims), out_shape=(ja...]
where the time goes in v2:
time: 47.6 us; the launch traced here: 47.3 us
  Pallas kernels  41.5 us (87%)
  local copies, waits for them, and re-layouts  5.12 us (11%)
  between operations  0.66 us (1%)
    pallas_call x1, Pallas kernels, per_device(): pl.pallas_call(functools.partial(kernel, nl, nh, nw, dims), out_shape=(ja...  41.5 us
    unnamed x15, local copies, waits for them, and re-layouts  5.12 us

profile of v2, /device:TPU:0, one launch (start us, length us, event | category | flops | bytes accessed | tf_op | source)
XLA Modules:
  0.0 47.3 jit_solution(730922733245487903)
XLA Ops:
  0.6 0.0 copy-start.4
  0.6 0.0 copy-start.5
  0.7 0.8 %copy.9.cnt_ref = s32[8,2,2]{2,1,0:T(2,128)S(1)} copy(s32[8,2,2]{0,2,1:T(2,128)} %param.10) | data formatting | bytes 256 | tf_op args[3]
  1.4 0.0 copy-done.4
  1.4 0.0 copy-done.5
  1.4 0.0 copy-start
  1.4 0.8 %copy-done = f32[3,8,2,2,128]{4,3,2,1,0:T(2,128)S(1)} copy-done((f32[3,8,2,2,128]{4,3,2,1,0:T(2,128)S(1)}, f32[3,8,2,2,128]{4,3,2,1,0:T(2,128)}, u32[]{:S(2)}) %copy-start) | copy-done | bytes 49176
  2.2 0.0 copy-start.1
  2.2 0.8 %copy-done.1 = f32[3,8,2,2,128]{4,3,2,1,0:T(2,128)S(1)} copy-done((f32[3,8,2,2,128]{4,3,2,1,0:T(2,128)S(1)}, f32[3,8,2,2,128]{4,3,2,1,0:T(2,128)}, u32[]{:S(2)}) %copy-start.1) | copy-done | bytes 49176
  3.0 0.0 copy-start.2
  3.0 0.7 %copy-done.2 = f32[8,2,2,128]{3,2,1,0:T(2,128)S(1)} copy-done((f32[8,2,2,128]{3,2,1,0:T(2,128)S(1)}, f32[8,2,2,128]{3,2,1,0:T(2,128)}, u32[]{:S(2)}) %copy-start.2) | copy-done | bytes 16408
  3.8 0.0 copy-start.3
  3.8 0.7 %copy-done.3 = s32[8,2,2,128]{3,2,1,0:T(2,128)S(1)} copy-done((s32[8,2,2,128]{3,2,1,0:T(2,128)S(1)}, s32[8,2,2,128]{3,2,1,0:T(2,128)}, u32[]{:S(2)}) %copy-start.3) | copy-done | bytes 16408
  4.5 41.5 %shard_map.86 = (f32[8,64,128]{2,1,0:T(8,128)S(1)}, f32[3,256]{1,0:T(4,128)S(1)}) custom-call(f32[3,8,2,2,128]{4,3,2,1,0:T(2,128)S(1)} %copy-done, f32[3,8,2,2,128]{4,3,2,1,0:T(2,128)S(1)} %copy-done.1, f32[8,2,2,128]{3,2,1,0:T(2,128)S(1)} %copy-done.2, s32[8,2,2]{2,1,0:T(2,128)S(1)} %copy.9.cnt_ref, s32[8,2,2,128]{3,2,1,0:T(2,128)S(1)} %copy-done.3, ...), custom_call_target="tpu_custom_call" | custom-call | tf_op jit(solution)/shard_map/pallas_call | solution.py:544
  46.0 0.7 %copy.13 = f32[8,1,1,64,128]{4,3,2,1,0:T(8,128)} copy(f32[8,1,1,64,128]{4,3,2,1,0:T(8,128)S(1)} %bitcast.4) | data formatting | bytes 524288
  46.7 0.6 %copy.14 = f32[3,256]{1,0:T(4,128)} copy(f32[3,256]{1,0:T(4,128)S(1)} %get-tuple-element.11) | data formatting | bytes 6144
Async XLA Ops:
  0.6 0.8 %copy-start.4 = (f32[3,256]{1,0:T(4,128)S(1)}, f32[3,256]{1,0:T(4,128)}, u32[]{:S(2)}) copy-start(f32[3,256]{1,0:T(4,128)} %flu_ref.1) | copy-start | bytes 9220
  0.6 0.8 %copy-start.5 = (s32[1,1,1,32,1]{3,4,2,1,0:T(1,128)S(1)}, s32[1,1,1,32,1]{3,4,2,1,0:T(1,128)}, u32[]{:S(2)}) copy-start(s32[1,1,1,32,1]{3,4,2,1,0:T(1,128)} %param.13) | copy-start | bytes 388
  1.4 0.8 %copy-start = (f32[3,8,2,2,128]{4,3,2,1,0:T(2,128)S(1)}, f32[3,8,2,2,128]{4,3,2,1,0:T(2,128)}, u32[]{:S(2)}) copy-start(f32[3,8,2,2,128]{4,3,2,1,0:T(2,128)} %pos_ref.1) | copy-start | bytes 147460
  2.2 0.8 %copy-start.1 = (f32[3,8,2,2,128]{4,3,2,1,0:T(2,128)S(1)}, f32[3,8,2,2,128]{4,3,2,1,0:T(2,128)}, u32[]{:S(2)}) copy-start(f32[3,8,2,2,128]{4,3,2,1,0:T(2,128)} %vel_ref.1) | copy-start | bytes 147460
  3.0 0.7 %copy-start.2 = (f32[8,2,2,128]{3,2,1,0:T(2,128)S(1)}, f32[8,2,2,128]{3,2,1,0:T(2,128)}, u32[]{:S(2)}) copy-start(f32[8,2,2,128]{3,2,1,0:T(2,128)} %rad_ref.1) | copy-start | bytes 49156
  3.8 0.7 %copy-start.3 = (s32[8,2,2,128]{3,2,1,0:T(2,128)S(1)}, s32[8,2,2,128]{3,2,1,0:T(2,128)}, u32[]{:S(2)}) copy-start(s32[8,2,2,128]{3,2,1,0:T(2,128)} %cell_ref.1) | copy-start | bytes 49156

commit v3 on v2

--- a/solution.py
+++ b/solution.py
@@ -49,8 +49,9 @@
 
 def kernel(
     nl, nh, nw, dims,
-    pos_ref, vel_ref, rad_ref, cnt_ref, cell_ref, flu_ref, plan_ref,
+    pos_hbm, vel_hbm, rad_hbm, cnt_hbm, cell_hbm, flu_hbm, plan_hbm,
     moved_ref, fnext_ref,
+    pos_ref, vel_ref, rad_ref, cnt_ref, cell_ref, flu_ref, plan_ref, load_sem,
     xr, vr, ur, accr, lv, xp, hl, hh, hw, lt, rr, pc, gg, tc, oh, ft, pb, pr,
     out0, out1, out2, in0, in1, in2,
     halo_send, halo_recv, grp_send, grp_recv, a2a_send, a2a_recv,
@@ -64,6 +65,15 @@
     me_w = lax.axis_index("wd")
     me_g = me_h * nw + me_w
 
+    loads = []
+    for k, (source, target) in enumerate((
+        (pos_hbm, pos_ref), (vel_hbm, vel_ref), (rad_hbm, rad_ref), (cnt_hbm, cnt_ref),
+        (cell_hbm, cell_ref), (flu_hbm, flu_ref), (plan_hbm, plan_ref),
+    )):
+        loads.append(pltpu.make_async_copy(source, target, load_sem.at[k]))
+    for load in loads:
+        load.start()
+
     barrier = pltpu.get_barrier_semaphore()
 
     def len_peer(k):
@@ -83,6 +93,10 @@
 
     row = lax.broadcasted_iota(jnp.int32, (8, 128), 0)
     lane = lax.broadcasted_iota(jnp.int32, (1, 128), 1)
+    layer_lane = lax.broadcasted_iota(jnp.int32, (1, gl), 1)
+
+    for load in loads:
+        load.wait()
 
     def load_layer(l, _):
         for h in range(gh):
@@ -94,7 +108,9 @@
                     xr[b, c : c + 1, :] = pos_ref[c, l, h, w : w + 1, :]
                     vr[b, c : c + 1, :] = vel_ref[c, l, h, w : w + 1, :]
                 xr[b, 3:4, :] = rad_ref[l, h, w : w + 1, :]
-                live = lane < cnt_ref[l, h, w]
+                numbers = cnt_ref[h, w : w + 1, :].astype(F32)
+                number = jnp.sum(jnp.where(layer_lane == l, numbers, 0.0), axis=1, keepdims=True)
+                live = lane.astype(F32) < number
                 lv[b] = jnp.broadcast_to(jnp.where(live, 1.0, 0.0), (8, 128))
                 xp[0, l, h, w] = jnp.where((lv[b] > 0.5) | (row >= 3), xr[b], PARK)
         return 0
@@ -208,31 +224,41 @@
         return jnp.where(row < 3, tile + off, 0.0)
 
     zero = jnp.zeros((8, 128), F32)
-    part_row = lax.broadcasted_iota(jnp.int32, (64, 384), 0)
-    part_of = part_row // 8
-    spread_out = jnp.where(
-        (lax.rem(part_row, 8) == lax.broadcasted_iota(jnp.int32, (64, 384), 1) // 128)
-        & ((part_of == 0) | (part_of == 2) | (part_of == 5)),
-        1.0, 0.0).astype(BF16)
+    part_row = lax.broadcasted_iota(jnp.int32, (32, 384), 0)
+    part_comp = lax.broadcasted_iota(jnp.int32, (32, 384), 1) // 128
+    spread_out = jnp.where((part_row == part_comp) | (part_row == part_comp + 16) | (part_row == part_comp + 27), 1.0, 0.0).astype(BF16)
+
+    def rows_of(*values):
+        out = zero
+        for k, value in enumerate(values):
+            if value is not None:
+                out = jnp.where(row == k, value, out)
+        return out
+
+    def halves(place):
+        return split3(place) + (split3(jnp.sum(place * place, axis=0, keepdims=True)),)
 
     def right_side(t, index, tile, place):
-        norm = jnp.sum(place * place, axis=0, keepdims=True)
-        h, m, l = split3(jnp.where(row < 3, 2.0 * place, jnp.where(row == 3, 1.0, jnp.where(row == 4, norm, 0.0))))
-        left = jnp.concatenate([h, m, h, m, l, h, zero, zero], axis=0)
-        rr[index, :, 0:128] = left.astype(BF16)
+        h, m, l, (nh_, nm_, nl_) = halves(place)
+        first = jnp.where(row < 3, 2.0 * h, rows_of(None, None, None, 1.0, nh_, None, None, 1.0))
+        second = jnp.where(row < 3, 2.0 * m, jnp.where(row == 3, pltpu.roll(2.0 * l, 1, 0), rows_of(None, None, None, None, nm_)))
+        third = jnp.where(row < 3, 2.0 * h, rows_of(None, None, None, 1.0, None, None, None, nl_))
+        fourth = jnp.where(row < 3, 2.0 * m, jnp.where(row < 6, pltpu.roll(2.0 * h, 3, 0), pltpu.roll(2.0 * l, 6, 0)))
+        rr[index, :, 0:128] = jnp.concatenate([first, second, third, fourth], axis=0).astype(BF16)
         if t == 0:
-            rh, rm, rl = split3(tile[3:4])
-            reach = jnp.where(row < 3, 1.0, jnp.where(row == 3, rh, jnp.where(row == 4, rm, jnp.where(row == 5, rl, 0.0))))
-            right = jnp.concatenate([zero] * 6 + [reach, zero], axis=0)
-            rr[index, :, 128:256] = right.astype(BF16)
+            rh, rm, _ = split3(tile[3:4])
+            reach = [rows_of(None, None, None, None, None, 1.0, rh), rows_of(None, None, None, None, None, None, rm),
+                     rows_of(None, None, None, None, None, 1.0), zero]
+            rr[index, :, 128:256] = jnp.concatenate(reach, axis=0).astype(BF16)
 
     def left_side(index, tile, place):
-        norm = jnp.sum(place * place, axis=0, keepdims=True)
-        h, m, l = split3(jnp.where(row < 3, place, jnp.where(row == 3, -norm, jnp.where(row == 4, -1.0, 0.0))))
-        rh, rm, rl = split3(tile[3:4])
-        reach = jnp.where(row == 0, rh, jnp.where(row == 1, rm, jnp.where(row == 2, rl, jnp.where(row < 6, 1.0, 0.0))))
-        full = jnp.concatenate([h, h, m, m, h, l, reach, zero], axis=0)
-        left = full.T.astype(BF16)
+        h, m, l, (nh_, nm_, nl_) = halves(place)
+        rh, rm, _ = split3(tile[3:4])
+        first = jnp.where(row < 3, h, rows_of(None, None, None, -nh_, -1.0, rh, 1.0, -nl_))
+        third = jnp.where(row < 3, m, rows_of(None, None, None, -nm_, None, rm, None, -1.0))
+        second = jnp.where(row == 3, pltpu.roll(h, 1, 0), first)
+        fourth = jnp.where(row < 3, m, jnp.where(row < 6, pltpu.roll(l, 3, 0), pltpu.roll(h, 6, 0)))
+        left = jnp.concatenate([first, second, third, fourth], axis=0).astype(BF16).T
         lt[index] = left
         pc[index] = dot(left, spread_out)
 
@@ -525,11 +551,14 @@
     blocks = gl * (gh * gw + 2 * (gh - 1) * gw + 2 * gh * (gw - 1)) + 2 * (gl - 1) * gh * gw + halos
     vmem = pltpu.VMEM
     scratch = [
+        vmem(positions.shape, F32), vmem(velocities.shape, F32), vmem(radius.shape, F32), vmem((gh, gw, gl), jnp.int32),
+        vmem(cell_index.shape, jnp.int32), vmem(fluid_velocity.shape, F32), vmem((1, bins), jnp.int32),
+        pltpu.SemaphoreType.DMA((7,)),
         vmem((bins, 8, 128), F32), vmem((bins, 8, 128), F32), vmem((bins, 8, 128), F32),
         vmem((bins, 8, 128), F32), vmem((bins, 8, 128), F32),
         vmem((2, gl, gh, gw, 8, 128), F32),
         vmem((2, sl, gh, gw, 8, 128), F32), vmem((2, sh, gl, gw, 8, 128), F32), vmem((2, sw, gl, gh, 8, 128), F32),
-        vmem((bins + halos, 128, 64), BF16), vmem((bins, 64, 256), BF16), vmem((bins + halos, 128, 384), F32),
+        vmem((bins + halos, 128, 32), BF16), vmem((bins, 32, 256), BF16), vmem((bins + halos, 128, 384), F32),
         vmem((bins, 32, 128), F32), vmem((blocks, 128, 128), F32),
         vmem((gl, 128, gh * gw * 128), BF16),
         vmem((groups, 8, 128), F32), vmem((groups, 8, 128), F32), vmem((max(1, groups - 1), 8, 128), F32),
@@ -540,20 +569,20 @@
         pltpu.SemaphoreType.DMA((3, nl)), pltpu.SemaphoreType.DMA((3, nl)),
     ]
     in_vmem = pl.BlockSpec(memory_space=pltpu.VMEM)
-    in_smem = pl.BlockSpec(memory_space=pltpu.SMEM)
+    anywhere = pl.BlockSpec(memory_space=pl.ANY)
     moved, fluid_next = pl.pallas_call(
         functools.partial(kernel, nl, nh, nw, dims),
         out_shape=(
             jax.ShapeDtypeStruct((8, nl * cap, slots), F32),
             jax.ShapeDtypeStruct(fluid_velocity.shape, F32),
         ),
-        in_specs=[in_vmem, in_vmem, in_vmem, in_smem, in_vmem, in_vmem, in_vmem],
+        in_specs=[anywhere] * 7,
         out_specs=(in_vmem, in_vmem),
         scratch_shapes=scratch,
         compiler_params=pltpu.CompilerParams(
-            collective_id=0, has_side_effects=True, vmem_limit_bytes=48 * 1024 * 1024
+            collective_id=0, has_side_effects=True, vmem_limit_bytes=56 * 1024 * 1024
         ),
-    )(positions, velocities, radius, counts, cell_index, fluid_velocity, plan.reshape(1, bins))
+    )(positions, velocities, radius, counts.transpose(1, 2, 0), cell_index, fluid_velocity, plan.reshape(1, bins))
     return moved.reshape(8, 1, 1, nl * cap, slots), fluid_next
 
 

time: 47.6 us -> 44.1 us (0.926)
  local copies, waits for them, and re-layouts: 5.12 us -> 2.27 us
  Pallas kernels: 41.5 us -> 41 us
    unnamed x15 -> x4, local copies, waits for them, and re-layouts: 5.12 us -> 2.27 us
    pallas_call x1, Pallas kernels: 41.5 us -> 41 us  [per_device(): pl.pallas_call(functools.partial(kernel, nl, nh, nw, dims), out_shape=(ja...]
where the time goes in v3:
time: 44.1 us; the launch traced here: 43.9 us
  Pallas kernels  41 us (93%)
  local copies, waits for them, and re-layouts  2.27 us (5%)
  between operations  0.65 us (1%)
    pallas_call x1, Pallas kernels, per_device(): pl.pallas_call(functools.partial(kernel, nl, nh, nw, dims), out_shape=(ja...  41 us
    unnamed x4, local copies, waits for them, and re-layouts  2.27 us

profile of v3, /device:TPU:0, one launch (start us, length us, event | category | flops | bytes accessed | tf_op | source)
XLA Modules:
  0.0 43.9 jit_solution(10733057504349046890)
XLA Ops:
  0.6 41.0 %shard_map.86 = (f32[8,64,128]{2,1,0:T(8,128)}, f32[3,256]{1,0:T(4,128)}) custom-call(f32[3,8,2,2,128]{4,3,2,1,0:T(2,128)} %pos_hbm.1, f32[3,8,2,2,128]{4,3,2,1,0:T(2,128)} %vel_hbm.1, f32[8,2,2,128]{3,2,1,0:T(2,128)} %rad_hbm.1, s32[2,2,8]{2,1,0:T(2,128)} %bitcast.6, s32[8,2,2,128]{3,2,1,0:T(2,128)} %cell_hbm.1, f32[3,256]{1,0:T(4,128)} %flu_hbm.1, ...), custom_call_target="tpu_custom_call" | custom-call | tf_op jit(solution)/shard_map/pallas_call | solution.py:573
  41.6 0.0 copy-start
  41.6 1.7 %copy.12 = f32[8,1,1,64,128]{4,3,2,1,0:T(8,128)} copy(f32[8,1,1,64,128]{4,3,2,1,0:T(8,128)} %bitcast.5) | data formatting | bytes 524288
  43.3 0.0 copy-done
  43.3 0.6 %copy.13 = f32[3,256]{1,0:T(4,128)} copy(f32[3,256]{1,0:T(4,128)S(1)} %copy-done) | data formatting | bytes 6144
Async XLA Ops:
  41.6 1.7 %copy-start = (f32[3,256]{1,0:T(4,128)S(1)}, f32[3,256]{1,0:T(4,128)}, u32[]{:S(2)}) copy-start(f32[3,256]{1,0:T(4,128)} %get-tuple-element.11) | copy-start | bytes 9220

commit v4 on v3

--- a/solution.py
+++ b/solution.py
@@ -251,7 +251,7 @@
                      rows_of(None, None, None, None, None, 1.0), zero]
             rr[index, :, 128:256] = jnp.concatenate(reach, axis=0).astype(BF16)
 
-    def left_side(index, tile, place):
+    def left_side(tile, place):
         h, m, l, (nh_, nm_, nl_) = halves(place)
         rh, rm, _ = split3(tile[3:4])
         first = jnp.where(row < 3, h, rows_of(None, None, None, -nh_, -1.0, rh, 1.0, -nl_))
@@ -259,24 +259,23 @@
         second = jnp.where(row == 3, pltpu.roll(h, 1, 0), first)
         fourth = jnp.where(row < 3, m, jnp.where(row < 6, pltpu.roll(l, 3, 0), pltpu.roll(h, 6, 0)))
         left = jnp.concatenate([first, second, third, fourth], axis=0).astype(BF16).T
-        lt[index] = left
-        pc[index] = dot(left, spread_out)
-
-    def push(t, target, source, block):
+        return left, dot(left, spread_out)
+
+    def push(t, target, source, columns, block):
         if t == 0:
-            both = dot(lt[source], rr[target])
+            both = dot(source, rr[target])
             dist = both[:, :128]
             inv = pl.reciprocal(both[:, 128:], approx=False)
             inv = inv * inv
             tc[block] = inv
         else:
-            dist = dot(lt[source], rr[target, :, 0:128])
+            dist = dot(source, rr[target, :, 0:128])
             inv = tc[block]
         e = jnp.exp(dist * inv)
         acc = [None] * 4
         for k in range(16):
             piece = e[8 * k : 8 * k + 8]
-            terms = [piece * pc[source, 8 * k : 8 * k + 8, 128 * c : 128 * c + 128] for c in range(3)] + [piece]
+            terms = [piece * columns[8 * k : 8 * k + 8, 128 * c : 128 * c + 128] for c in range(3)] + [piece]
             acc = terms if k == 0 else [a + b for a, b in zip(acc, terms)]
         return jnp.concatenate(acc, axis=0)
 
@@ -299,7 +298,7 @@
                     tile = xp[t, l, h, w]
                     place = coords(tile, (l, h, w))
                     right_side(t, b, tile, place)
-                    left_side(b, tile, place)
+                    lt[b], pc[b] = left_side(tile, place)
             return 0
 
         lax.fori_loop(0, gl, one, 0)
@@ -309,7 +308,7 @@
             base = l * layer
             sums = [None] * layer
             for n_, (i, j) in enumerate(near):
-                got = push(t, base + i, base + j, l * per_layer + n_)
+                got = push(t, base + i, lt[base + j], pc.at[base + j], l * per_layer + n_)
                 sums[i] = got if sums[i] is None else sums[i] + got
             for n_ in range(layer):
                 gg[base + n_] = sums[n_]
@@ -322,8 +321,8 @@
             ups, downs = [], []
             for n_ in range(layer):
                 block = base_len + 2 * (base + n_)
-                ups.append(push(t, base + layer + n_, base + n_, block))
-                downs.append(push(t, base + n_, base + layer + n_, block + 1))
+                ups.append(push(t, base + layer + n_, lt[base + n_], pc.at[base + n_], block))
+                downs.append(push(t, base + n_, lt[base + layer + n_], pc.at[base + layer + n_], block + 1))
             for n_ in range(layer):
                 gg[base + n_] += downs[n_]
                 gg[base + layer + n_] += ups[n_]
@@ -338,9 +337,9 @@
             for h in range(gh):
                 for w in range(gw):
                     tile = hl[t, s, h, w]
-                    left_side(at + h * gw + w, tile, coords(tile, (coord, h, w)))
-            for n_ in range(layer):
-                sums.append(push(t, face * layer + n_, at + n_, base_halo + at - bins + n_))
+                    source, columns = left_side(tile, coords(tile, (coord, h, w)))
+                    n_ = h * gw + w
+                    sums.append(push(t, face * layer + n_, source, columns, base_halo + at - bins + n_))
             for n_ in range(layer):
                 gg[face * layer + n_] += sums[n_]
             at += layer
@@ -356,14 +355,11 @@
                         for y in range(across):
                             tile = ref[t, s, l, y]
                             place = coords(tile, (l, coord, y) if a == 1 else (l, y, coord))
-                            left_side(at + l * across + y, tile, place)
-                    for q in range(step):
-                        l = p * step + q
-                        for y in range(across):
+                            source, columns = left_side(tile, place)
                             n_ = at + l * across + y
                             target = l * layer + (face * gw + y if a == 1 else y * gw + face)
                             targets.append(target)
-                            sums.append(push(t, target, n_, base_halo + n_ - bins))
+                            sums.append(push(t, target, source, columns, base_halo + n_ - bins))
                     for target, got in zip(targets, sums):
                         gg[target] += got
                     return 0
@@ -558,7 +554,7 @@
         vmem((bins, 8, 128), F32), vmem((bins, 8, 128), F32),
         vmem((2, gl, gh, gw, 8, 128), F32),
         vmem((2, sl, gh, gw, 8, 128), F32), vmem((2, sh, gl, gw, 8, 128), F32), vmem((2, sw, gl, gh, 8, 128), F32),
-        vmem((bins + halos, 128, 32), BF16), vmem((bins, 32, 256), BF16), vmem((bins + halos, 128, 384), F32),
+        vmem((bins, 128, 32), BF16), vmem((bins, 32, 256), BF16), vmem((bins, 128, 384), F32),
         vmem((bins, 32, 128), F32), vmem((blocks, 128, 128), F32),
         vmem((gl, 128, gh * gw * 128), BF16),
         vmem((groups, 8, 128), F32), vmem((groups, 8, 128), F32), vmem((max(1, groups - 1), 8, 128), F32),

time: 44.1 us -> 43.2 us (0.980)
  Pallas kernels: 41 us -> 40.1 us
    pallas_call x1, Pallas kernels: 41 us -> 40.1 us  [per_device(): pl.pallas_call(functools.partial(kernel, nl, nh, nw, dims), out_shape=(ja...]
where the time goes in v4:
time: 43.2 us; the launch traced here: 43 us
  Pallas kernels  40.1 us (93%)
  local copies, waits for them, and re-layouts  2.27 us (5%)
  between operations  0.65 us (2%)
    pallas_call x1, Pallas kernels, per_device(): pl.pallas_call(functools.partial(kernel, nl, nh, nw, dims), out_shape=(ja...  40.1 us
    unnamed x4, local copies, waits for them, and re-layouts  2.27 us

profile of v4, /device:TPU:0, one launch (start us, length us, event | category | flops | bytes accessed | tf_op | source)
XLA Modules:
  0.0 43.0 jit_solution(18102204800403536326)
XLA Ops:
  0.6 40.1 %shard_map.86 = (f32[8,64,128]{2,1,0:T(8,128)}, f32[3,256]{1,0:T(4,128)}) custom-call(f32[3,8,2,2,128]{4,3,2,1,0:T(2,128)} %pos_hbm.1, f32[3,8,2,2,128]{4,3,2,1,0:T(2,128)} %vel_hbm.1, f32[8,2,2,128]{3,2,1,0:T(2,128)} %rad_hbm.1, s32[2,2,8]{2,1,0:T(2,128)} %bitcast.6, s32[8,2,2,128]{3,2,1,0:T(2,128)} %cell_hbm.1, f32[3,256]{1,0:T(4,128)} %flu_hbm.1, ...), custom_call_target="tpu_custom_call" | custom-call | tf_op jit(solution)/shard_map/pallas_call | solution.py:569
  40.8 0.0 copy-start
  40.8 1.7 %copy.12 = f32[8,1,1,64,128]{4,3,2,1,0:T(8,128)} copy(f32[8,1,1,64,128]{4,3,2,1,0:T(8,128)} %bitcast.5) | data formatting | bytes 524288
  42.4 0.0 copy-done
  42.4 0.6 %copy.13 = f32[3,256]{1,0:T(4,128)} copy(f32[3,256]{1,0:T(4,128)S(1)} %copy-done) | data formatting | bytes 6144
Async XLA Ops:
  40.8 1.7 %copy-start = (f32[3,256]{1,0:T(4,128)S(1)}, f32[3,256]{1,0:T(4,128)}, u32[]{:S(2)}) copy-start(f32[3,256]{1,0:T(4,128)} %get-tuple-element.11) | copy-start | bytes 9220

commit v5 on v4

--- a/solution.py
+++ b/solution.py
@@ -346,7 +346,7 @@
         for a, across in ((1, gw), (2, gh)):
             ref = plans[a][1]
             for s, (partner, face, coord, exists) in enumerate(plans[a][2]):
-                step = 2 if gl % 2 == 0 else 1
+                step = 4 if gl % 4 == 0 else 1
 
                 def one(p, _, ref=ref, s=s, face=face, coord=coord, a=a, across=across, at=at, step=step):
                     targets, sums = [], []

time: 43.2 us -> 41.4 us (0.958)
  Pallas kernels: 40.1 us -> 38.3 us
    pallas_call x1, Pallas kernels: 40.1 us -> 38.3 us  [per_device(): pl.pallas_call(functools.partial(kernel, nl, nh, nw, dims), out_shape=(ja...]
where the time goes in v5:
time: 41.4 us; the launch traced here: 41.2 us
  Pallas kernels  38.3 us (93%)
  local copies, waits for them, and re-layouts  2.27 us (5%)
  between operations  0.65 us (2%)
    pallas_call x1, Pallas kernels, per_device(): pl.pallas_call(functools.partial(kernel, nl, nh, nw, dims), out_shape=(ja...  38.3 us
    unnamed x4, local copies, waits for them, and re-layouts  2.27 us

profile of v5, /device:TPU:0, one launch (start us, length us, event | category | flops | bytes accessed | tf_op | source)
XLA Modules:
  0.0 41.2 jit_solution(12073531531233492412)
XLA Ops:
  0.6 38.3 %shard_map.86 = (f32[8,64,128]{2,1,0:T(8,128)}, f32[3,256]{1,0:T(4,128)}) custom-call(f32[3,8,2,2,128]{4,3,2,1,0:T(2,128)} %pos_hbm.1, f32[3,8,2,2,128]{4,3,2,1,0:T(2,128)} %vel_hbm.1, f32[8,2,2,128]{3,2,1,0:T(2,128)} %rad_hbm.1, s32[2,2,8]{2,1,0:T(2,128)} %bitcast.6, s32[8,2,2,128]{3,2,1,0:T(2,128)} %cell_hbm.1, f32[3,256]{1,0:T(4,128)} %flu_hbm.1, ...), custom_call_target="tpu_custom_call" | custom-call | tf_op jit(solution)/shard_map/pallas_call | solution.py:569
  38.9 0.0 copy-start
  38.9 1.7 %copy.12 = f32[8,1,1,64,128]{4,3,2,1,0:T(8,128)} copy(f32[8,1,1,64,128]{4,3,2,1,0:T(8,128)} %bitcast.5) | data formatting | bytes 524288
  40.6 0.0 copy-done
  40.6 0.6 %copy.13 = f32[3,256]{1,0:T(4,128)} copy(f32[3,256]{1,0:T(4,128)S(1)} %copy-done) | data formatting | bytes 6144
Async XLA Ops:
  38.9 1.7 %copy-start = (f32[3,256]{1,0:T(4,128)S(1)}, f32[3,256]{1,0:T(4,128)}, u32[]{:S(2)}) copy-start(f32[3,256]{1,0:T(4,128)} %get-tuple-element.11) | copy-start | bytes 9220
